TPU v7x, 32 devices: a whole 2x2x4 slice. The times are simulated.
32 devices in a mesh: groups: 2 (over x), tm: 16 (over z, y, core).
Axes of the slice: x: 2, y: 2, z: 4, core: 2. Of those that a mesh axis runs over, the one named last changes fastest.
Arguments:
- queries: bfloat16 [12288, 2240], P(('groups', 'tm')), parts along dimension 0, may hold values from -40 to 40
- keys: bfloat16 [12288, 2240], P(('groups', 'tm')), parts along dimension 0, may hold values from -6 to 6
- values: bfloat16 [12288, 2240], P(('groups', 'tm')), parts along dimension 0, may hold values from -6 to 6
- cross_queries: bfloat16 [12288, 2240], P(('groups', 'tm')), parts along dimension 0, may hold values from -540 to 540
- prompt_keys: bfloat16 [32, 128, 2240], P(('groups', 'tm')), parts along dimension 0, may hold values from -6 to 6
- prompt_values: bfloat16 [32, 128, 2240], P(('groups', 'tm')), parts along dimension 0, may hold values from -6 to 6
- caption_keys: bfloat16 [256, 2240], P('groups'), parts along dimension 0, may hold values from -6 to 6
- caption_values: bfloat16 [256, 2240], P('groups'), parts along dimension 0, may hold values from -6 to 6
- span_start: int32 [32], P('groups'), parts along dimension 0, may hold values from 0 to 15, as said below
- span_end: int32 [32], P('groups'), parts along dimension 0, may hold values from 1 to 16
- prompt_tokens: int32 [32], P('groups'), parts along dimension 0, may hold values from 80 to 128, as said below
- region_mask: int32 [32, 3], P('groups'), parts along dimension 0, may hold values 0 or 1
- out_gain: float32 [2240], replicated, may hold values from 0.5 to 1.5
Outputs:
- self_mixed: bfloat16 [12288, 2240], P(('groups', 'tm')), parts along dimension 0
- cross_mixed: bfloat16 [12288, 2240], P(('groups', 'tm')), parts along dimension 0
There are 2 independent parts, one for each index of `groups`. A program takes and returns all parts, laid end to end along the dimension named above; an argument that names none is the same for every part. Nothing has to cross between parts.
Inputs may be any that keep to these rules, and one draw needn't show every extreme that they name: Prompt p applies to stretches span_start[p] to span_end[p] - 1, with p <= span_start[p] <= p + 1 and span_start[p] < span_end[p] <= p + 6; prompt 0 covers stretches 0 to 5. `prompt_tokens`: prompt 0 uses all 128 slots.
All inputs are finite; a program needn't handle non-finite values.
Results may differ from a plain program's by a relative error of at most 0.007.
Values may be sent and summed in bfloat16 or wider, within the bound.
No kernel may reach another device: no remote copies, remote signals or barrier semaphores. Data moves between devices by JAX's collectives and lax.ppermute only.
A program may use at most 128 MiB of HBM per device.

v0:
```python
import math

import jax
import jax.numpy as jnp
from jax import lax
from jax.sharding import PartitionSpec as P

HD = 32
SPAN = 6
PR_DEV = 1
PL = 128


def prefix(value, axis, join, neutral):
    place = lax.axis_index(axis)
    gathered = lax.all_gather(value.astype(jnp.bfloat16), axis)
    state = jnp.zeros_like(value) + jnp.asarray(neutral, value.dtype)

    def one(hop, state):
        return join(state, lax.dynamic_index_in_dim(gathered, hop, 0, False).astype(value.dtype))

    return lax.fori_loop(0, place, one, state)


def passed_along(block, axis, distance):
    devices = range(lax.axis_size(axis))
    route = [(i - distance, i) for i in devices if i - distance in devices]
    return lax.ppermute(block, axis, route)


def add_states(earlier, later):
    return earlier + later


def prompt_tiles(owner_id, stretch_id, span_start, span_end, prompt_tokens, region_mask):
    first_row = jnp.maximum(owner_id, 0) * PR_DEV
    begins = lax.dynamic_slice_in_dim(span_start, first_row, PR_DEV, 0)
    finish = lax.dynamic_slice_in_dim(span_end, first_row, PR_DEV, 0)
    counts = lax.dynamic_slice_in_dim(prompt_tokens, first_row, PR_DEV, 0)
    regions = lax.dynamic_slice_in_dim(region_mask, first_row, PR_DEV, 0)
    covers = (owner_id >= 0) & (begins <= stretch_id) & (stretch_id < finish)
    live_keys = jnp.arange(PL, dtype=jnp.int32)[None, :] < counts[:, None]
    visible_set = covers[:, None, None] & (regions[:, :, None] == 1) & live_keys[:, None, :]
    return jnp.transpose(visible_set, (1, 0, 2)).reshape(regions.shape[1], PR_DEV * PL)


def per_token(tile_mask, tok_rows):
    tile_count, key_count = tile_mask.shape
    spread_out = jnp.broadcast_to(
        tile_mask[:, None, :], (tile_count, tok_rows // tile_count, key_count)
    )
    return spread_out.reshape(tok_rows, key_count)


def attend_block(state_in, query_rows, block_keys, block_values, visible):
    run_max, run_sum, running = state_in
    tok_rows, head_count, head_size = query_rows.shape
    keys_three = block_keys.reshape(block_keys.shape[0], head_count, head_size)
    values_three = block_values.reshape(block_values.shape[0], head_count, head_size)
    scores = jnp.einsum(
        "rhd,khd->hrk", query_rows, keys_three, preferred_element_type=jnp.float32
    ) * head_size ** (-0.5)
    scores = jnp.where(visible[None], scores, -1e30)
    new_max = jnp.maximum(run_max, jnp.max(scores, axis=2))
    expo = jnp.where(visible[None], jnp.exp(scores - new_max[:, :, None]), 0.0)
    run_sum = jnp.sum(expo, axis=2)
    added = jnp.einsum(
        "hrk,khd->rhd", expo.astype(jnp.bfloat16), values_three, preferred_element_type=jnp.float32
    )
    running = added
    return (new_max, run_sum, running)


def empty_state(head_count, tok_rows):
    return (
        jnp.full((head_count, tok_rows), -1e30, jnp.float32),
        jnp.zeros((head_count, tok_rows), jnp.float32),
        jnp.zeros((tok_rows, head_count, HD), jnp.float32),
    )


def joined_attention(query_rows, all_keys, all_values, visible):
    tok_rows, head_count, head_size = query_rows.shape
    key_count = all_keys.shape[0]
    group = math.gcd(head_count, 10)
    group_count = head_count // group
    query_groups = jnp.transpose(
        query_rows.reshape(tok_rows, group_count, group, head_size), (1, 0, 2, 3)
    )
    key_groups = jnp.transpose(
        all_keys.reshape(key_count, group_count, group * head_size), (1, 0, 2)
    )
    value_groups = jnp.transpose(
        all_values.reshape(key_count, group_count, group * head_size), (1, 0, 2)
    )

    def one_group(packed):
        query_part, key_part, value_part = packed
        run_max, run_sum, running = attend_block(
            empty_state(group, tok_rows), query_part, key_part, value_part, visible
        )
        return running / jnp.transpose(run_sum)[:, :, None]

    mixed_groups = lax.map(one_group, (query_groups, key_groups, value_groups))
    return jnp.transpose(mixed_groups, (1, 0, 2, 3)).reshape(tok_rows, head_count * head_size)


def local(
    queries,
    keys,
    values,
    cross_queries,
    prompt_keys,
    prompt_values,
    caption_keys,
    caption_values,
    span_start,
    span_end,
    prompt_tokens,
    region_mask,
    out_gain,
):
    tok_rows, model_width = queries.shape
    head_count = model_width // HD
    stretch_id = lax.axis_index("tm")
    lifted_keys = jnp.maximum(keys, 0).reshape(tok_rows, head_count, HD)
    stretch_state = jnp.einsum(
        "rhd,rhe->hde",
        lifted_keys,
        values.reshape(tok_rows, head_count, HD),
        preferred_element_type=jnp.float32,
    )
    prior_state = prefix(
        stretch_state.reshape(head_count, HD * HD),
        "tm",
        add_states,
        jnp.zeros((head_count, HD * HD), jnp.float32),
    )
    whole_state = (prior_state.reshape(head_count, HD, HD) + stretch_state).astype(jnp.bfloat16)
    lifted_queries = jnp.maximum(queries, 0).reshape(tok_rows, head_count, HD)
    raw_mix = jnp.einsum(
        "rhd,hde->rhe", lifted_queries, whole_state, preferred_element_type=jnp.float32
    ).reshape(tok_rows, model_width)
    mean_square = jnp.mean(raw_mix * raw_mix, axis=-1, keepdims=True)
    self_mixed = (raw_mix * lax.rsqrt(mean_square + 1e-05) * out_gain[None, :]).astype(jnp.bfloat16)
    query_rows = cross_queries.reshape(tok_rows, head_count, HD)
    caption_seen = jnp.ones((tok_rows, caption_keys.shape[0]), dtype=bool)
    slot_count = prompt_keys.shape[0] * prompt_keys.shape[1]
    blocks = [(prompt_keys, prompt_values)]
    moving = (prompt_keys, prompt_values)
    for reach in range(1, SPAN):
        moving = passed_along((moving[0], moving[1]), "tm", 1)
        blocks.append(moving)
    block_keys = [blocks[reach][0].reshape(slot_count, model_width) for reach in range(SPAN)]
    block_values = [blocks[reach][1].reshape(slot_count, model_width) for reach in range(SPAN)]
    block_seen = [
        per_token(
            prompt_tiles(
                stretch_id - reach, stretch_id, span_start, span_end, prompt_tokens, region_mask
            ),
            tok_rows,
        )
        for reach in range(SPAN)
    ]
    all_keys = jnp.concatenate([caption_keys] + block_keys, axis=0)
    all_values = jnp.concatenate([caption_values] + block_values, axis=0)
    visible = jnp.concatenate([caption_seen] + block_seen, axis=1)
    cross_mixed = joined_attention(query_rows, all_keys, all_values, visible).astype(jnp.bfloat16)
    return (self_mixed, cross_mixed)


def solution(mesh):
    in_specs = (
        P(("groups", "tm"), None),
        P(("groups", "tm"), None),
        P(("groups", "tm"), None),
        P(("groups", "tm"), None),
        P(("groups", "tm"), None, None),
        P(("groups", "tm"), None, None),
        P("groups", None),
        P("groups", None),
        P("groups"),
        P("groups"),
        P("groups"),
        P("groups", None),
        P(),
    )
    out_specs = (P(("groups", "tm"), None), P(("groups", "tm"), None))
    return jax.shard_map(local, mesh=mesh, in_specs=in_specs, out_specs=out_specs, check_vma=False)
```

profile of v0, /device:TPU:24, one launch (start us, length us, event | category | flops | bytes accessed | tf_op | source)
XLA Modules:
  0.0 229.2 jit_solution(11526491504432644969)
XLA Ops:
  7.2 2.1 collective-permute-start
  9.3 3.5 %collective-permute-start.5 = (bf16[1,128,2240]{1,2,0:T(8,128)(2,1)}, bf16[1,128,2240]{1,2,0:T(8,128)(2,1)}, u32[]{:S(2)}, u32[]{:S(2)}) collective-permute-start(bf16[1,128,2240]{1,2,0:T(8,128)(2,1)} %param.21), channel_id=1, source_target_pairs={{0,1},{1,2},{2,3},{3,4},{4,5},{5,6},{6,7},{7,8},{8,9},{9,10},{10,1... | collective-permute-start | bytes 1720328 | tf_op jit(solution)/shard_map/ppermute | solution.py:28
  12.8 1.6 broadcast_maximum_fusion.2
  14.5 1.6 fusion.43
  16.1 1.7 copy.26
  31.0 2.0 constant_dynamic-update-slice_fusion.6
  32.9 2.0 constant_dynamic-update-slice_fusion.19
  34.9 1.9 constant_dynamic-update-slice_fusion.5
  37.8 1.9 collective-permute-start.1
  39.7 1.9 collective-permute-start.6
  41.7 1.3 broadcast_maximum_fusion.1
  43.0 13.3 %collective-permute-done.1 = bf16[1,128,2240]{1,2,0:T(8,128)(2,1)} collective-permute-done((bf16[1,128,2240]{1,2,0:T(8,128)(2,1)}, bf16[1,128,2240]{1,2,0:T(8,128)(2,1)}, u32[]{:S(2)}, u32[]{:S(2)}) %collective-permute-start.1) | collective-permute-done | bytes 573472 | tf_op jit(solution)/shard_map/ppermute | solution.py:28
  56.3 1.9 collective-permute-start.2
  58.8 6.8 %collective-permute-done.6 = bf16[1,128,2240]{1,2,0:T(8,128)(2,1)} collective-permute-done((bf16[1,128,2240]{1,2,0:T(8,128)(2,1)}, bf16[1,128,2240]{1,2,0:T(8,128)(2,1)}, u32[]{:S(2)}, u32[]{:S(2)}) %collective-permute-start.6) | collective-permute-done | bytes 573472 | tf_op jit(solution)/shard_map/ppermute | solution.py:28
  65.6 1.9 collective-permute-start.7
  68.2 1.6 copy.29
  69.9 1.8 collective-permute-done.2
  71.8 1.9 collective-permute-start.3
  73.8 4.2 %collective-permute-done.7 = bf16[1,128,2240]{1,2,0:T(8,128)(2,1)} collective-permute-done((bf16[1,128,2240]{1,2,0:T(8,128)(2,1)}, bf16[1,128,2240]{1,2,0:T(8,128)(2,1)}, u32[]{:S(2)}, u32[]{:S(2)}) %collective-permute-start.7) | collective-permute-done | bytes 573472 | tf_op jit(solution)/shard_map/ppermute | solution.py:28
  77.9 1.9 collective-permute-start.8
  79.9 1.9 constant_dynamic-update-slice_fusion.4
  81.8 2.0 constant_dynamic-update-slice_fusion.17
  83.8 2.0 constant_dynamic-update-slice_fusion.3
  85.8 1.9 collective-permute-start.4
  87.7 2.0 constant_dynamic-update-slice_fusion.16
  90.1 1.9 collective-permute-start.9
  92.0 2.0 constant_dynamic-update-slice_fusion.2
  94.0 1.9 constant_dynamic-update-slice_fusion.15
  98.7 5.1 %collective-permute-done.9 = bf16[1,128,2240]{1,2,0:T(8,128)(2,1)S(1)} collective-permute-done((bf16[1,128,2240]{1,2,0:T(8,128)(2,1)S(1)}, bf16[1,128,2240]{1,2,0:T(8,128)(2,1)S(1)}, u32[]{:S(2)}, u32[]{:S(2)}) %collective-permute-start.9) | collective-permute-done | bytes 573472 | tf_op jit(solution)/shard_map/ppermute | solution.py:28
  104.7 100.3 %while.21 = (s32[]{:T(128)}, bf16[7,384,10,32]{1,3,2,0:T(8,128)(2,1)}, bf16[7,896,320]{1,2,0:T(8,128)(2,1)}, pred[384,896]{1,0:T(8,128)(4,1)S(1)}, bf16[7,384,10...) while((s32[]{:T(128)}, bf16[7,384,10,32]{1,3,2,0:T(8,128)(2,1)}, ...), condition=%wide.region_6.7_spmd, body=%wide.region_3.6_spmd.sunk | while | flops 485249280 | bytes 46606416 | solution.py:104
  104.7 1.3 constant_dynamic-slice_fusion.3
  106.1 3.8 %fusion.59 = (f32[10,384]{1,0:T(8,128)S(1)}, f32[10,384,896]{2,1,0:T(8,128)S(1)}) fusion(pred[384,896]{1,0:T(8,128)(4,1)S(1)} %get-tuple-element.230, bf16[896,10,32]{0,2,1:T(8,128)(2,1)S(1)} %bitcast.111, bf16[7,384,10,32]{1,3,2,0:T(8,128)(2,1)} %get-tuple-element.231, s32[]{:T(128)} %get-tuple-element.220), kind=kOutput, calls=%fused_computation.3.clone.1 | convolution fusion | flops 230519040 | bytes 14941696 | tf_op jit(solution)/shard_map/while/body/eval_jaxpr/rhd,khd->hrk/dot_general | solution.py:60
  109.9 4.3 %fusion.60 = f32[10,384]{1,0:T(8,128)S(1)} fusion(f32[10,384,896]{2,1,0:T(8,128)S(1)} %get-tuple-element.190, f32[10,384]{1,0:T(8,128)S(1)} %broadcast_maximum_fusion.4, pred[384,896]{1,0:T(8,128)(4,1)S(1)} %get-tuple-element.230), kind=kLoop, calls=%fused_computation.4.clone.1 | loop fusion | flops 17199360 | bytes 14137344 | tf_op jit(solution)/shard_map/while/body/eval_jaxpr/reduce_sum | solution.py:66
  114.2 4.9 %fusion.61 = bf16[7,384,10,32]{1,3,2,0:T(8,128)(2,1)} fusion(bf16[7,384,10,32]{1,3,2,0:T(8,128)(2,1)} %get-tuple-element.221, s32[]{:T(128)} %get-tuple-element.220, bf16[896,10,32]{0,2,1:T(8,128)(2,1)S(1)} %bitcast.112, f32[10,384,896]{2,1,0:T(8,128)S(1)} %get-tuple-element.190, f32[10,384]{1,0:T(8,128)S(1)} %broadcast_maximum_fusion.4, ...), kind=kOutput, calls=%fused_computation.11.clone.1 | convolution fusion | flops 237527040 | bytes 15202816 | tf_op jit(solution)/shard_map/while/body/eval_jaxpr/hrk,khd->rhd/dot_general | solution.py:67
  119.1 1.3 constant_dynamic-slice_fusion.3
  120.4 3.8 %fusion.59 = (f32[10,384]{1,0:T(8,128)S(1)}, f32[10,384,896]{2,1,0:T(8,128)S(1)}) fusion(pred[384,896]{1,0:T(8,128)(4,1)S(1)} %get-tuple-element.230, bf16[896,10,32]{0,2,1:T(8,128)(2,1)S(1)} %bitcast.111, bf16[7,384,10,32]{1,3,2,0:T(8,128)(2,1)} %get-tuple-element.231, s32[]{:T(128)} %get-tuple-element.220), kind=kOutput, calls=%fused_computation.3.clone.1 | convolution fusion | flops 230519040 | bytes 14941696 | tf_op jit(solution)/shard_map/while/body/eval_jaxpr/rhd,khd->hrk/dot_general | solution.py:60
  124.2 4.3 %fusion.60 = f32[10,384]{1,0:T(8,128)S(1)} fusion(f32[10,384,896]{2,1,0:T(8,128)S(1)} %get-tuple-element.190, f32[10,384]{1,0:T(8,128)S(1)} %broadcast_maximum_fusion.4, pred[384,896]{1,0:T(8,128)(4,1)S(1)} %get-tuple-element.230), kind=kLoop, calls=%fused_computation.4.clone.1 | loop fusion | flops 17199360 | bytes 14137344 | tf_op jit(solution)/shard_map/while/body/eval_jaxpr/reduce_sum | solution.py:66
  128.5 4.9 %fusion.61 = bf16[7,384,10,32]{1,3,2,0:T(8,128)(2,1)} fusion(bf16[7,384,10,32]{1,3,2,0:T(8,128)(2,1)} %get-tuple-element.221, s32[]{:T(128)} %get-tuple-element.220, bf16[896,10,32]{0,2,1:T(8,128)(2,1)S(1)} %bitcast.112, f32[10,384,896]{2,1,0:T(8,128)S(1)} %get-tuple-element.190, f32[10,384]{1,0:T(8,128)S(1)} %broadcast_maximum_fusion.4, ...), kind=kOutput, calls=%fused_computation.11.clone.1 | convolution fusion | flops 237527040 | bytes 15202816 | tf_op jit(solution)/shard_map/while/body/eval_jaxpr/hrk,khd->rhd/dot_general | solution.py:67
  133.4 1.3 constant_dynamic-slice_fusion.3
  134.7 3.8 %fusion.59 = (f32[10,384]{1,0:T(8,128)S(1)}, f32[10,384,896]{2,1,0:T(8,128)S(1)}) fusion(pred[384,896]{1,0:T(8,128)(4,1)S(1)} %get-tuple-element.230, bf16[896,10,32]{0,2,1:T(8,128)(2,1)S(1)} %bitcast.111, bf16[7,384,10,32]{1,3,2,0:T(8,128)(2,1)} %get-tuple-element.231, s32[]{:T(128)} %get-tuple-element.220), kind=kOutput, calls=%fused_computation.3.clone.1 | convolution fusion | flops 230519040 | bytes 14941696 | tf_op jit(solution)/shard_map/while/body/eval_jaxpr/rhd,khd->hrk/dot_general | solution.py:60
  138.5 4.3 %fusion.60 = f32[10,384]{1,0:T(8,128)S(1)} fusion(f32[10,384,896]{2,1,0:T(8,128)S(1)} %get-tuple-element.190, f32[10,384]{1,0:T(8,128)S(1)} %broadcast_maximum_fusion.4, pred[384,896]{1,0:T(8,128)(4,1)S(1)} %get-tuple-element.230), kind=kLoop, calls=%fused_computation.4.clone.1 | loop fusion | flops 17199360 | bytes 14137344 | tf_op jit(solution)/shard_map/while/body/eval_jaxpr/reduce_sum | solution.py:66
  142.8 4.9 %fusion.61 = bf16[7,384,10,32]{1,3,2,0:T(8,128)(2,1)} fusion(bf16[7,384,10,32]{1,3,2,0:T(8,128)(2,1)} %get-tuple-element.221, s32[]{:T(128)} %get-tuple-element.220, bf16[896,10,32]{0,2,1:T(8,128)(2,1)S(1)} %bitcast.112, f32[10,384,896]{2,1,0:T(8,128)S(1)} %get-tuple-element.190, f32[10,384]{1,0:T(8,128)S(1)} %broadcast_maximum_fusion.4, ...), kind=kOutput, calls=%fused_computation.11.clone.1 | convolution fusion | flops 237527040 | bytes 15202816 | tf_op jit(solution)/shard_map/while/body/eval_jaxpr/hrk,khd->rhd/dot_general | solution.py:67
  147.7 1.3 constant_dynamic-slice_fusion.3
  149.1 3.8 %fusion.59 = (f32[10,384]{1,0:T(8,128)S(1)}, f32[10,384,896]{2,1,0:T(8,128)S(1)}) fusion(pred[384,896]{1,0:T(8,128)(4,1)S(1)} %get-tuple-element.230, bf16[896,10,32]{0,2,1:T(8,128)(2,1)S(1)} %bitcast.111, bf16[7,384,10,32]{1,3,2,0:T(8,128)(2,1)} %get-tuple-element.231, s32[]{:T(128)} %get-tuple-element.220), kind=kOutput, calls=%fused_computation.3.clone.1 | convolution fusion | flops 230519040 | bytes 14941696 | tf_op jit(solution)/shard_map/while/body/eval_jaxpr/rhd,khd->hrk/dot_general | solution.py:60
  152.9 4.3 %fusion.60 = f32[10,384]{1,0:T(8,128)S(1)} fusion(f32[10,384,896]{2,1,0:T(8,128)S(1)} %get-tuple-element.190, f32[10,384]{1,0:T(8,128)S(1)} %broadcast_maximum_fusion.4, pred[384,896]{1,0:T(8,128)(4,1)S(1)} %get-tuple-element.230), kind=kLoop, calls=%fused_computation.4.clone.1 | loop fusion | flops 17199360 | bytes 14137344 | tf_op jit(solution)/shard_map/while/body/eval_jaxpr/reduce_sum | solution.py:66
  157.2 4.9 %fusion.61 = bf16[7,384,10,32]{1,3,2,0:T(8,128)(2,1)} fusion(bf16[7,384,10,32]{1,3,2,0:T(8,128)(2,1)} %get-tuple-element.221, s32[]{:T(128)} %get-tuple-element.220, bf16[896,10,32]{0,2,1:T(8,128)(2,1)S(1)} %bitcast.112, f32[10,384,896]{2,1,0:T(8,128)S(1)} %get-tuple-element.190, f32[10,384]{1,0:T(8,128)S(1)} %broadcast_maximum_fusion.4, ...), kind=kOutput, calls=%fused_computation.11.clone.1 | convolution fusion | flops 237527040 | bytes 15202816 | tf_op jit(solution)/shard_map/while/body/eval_jaxpr/hrk,khd->rhd/dot_general | solution.py:67
  162.1 1.3 constant_dynamic-slice_fusion.3
  163.4 3.8 %fusion.59 = (f32[10,384]{1,0:T(8,128)S(1)}, f32[10,384,896]{2,1,0:T(8,128)S(1)}) fusion(pred[384,896]{1,0:T(8,128)(4,1)S(1)} %get-tuple-element.230, bf16[896,10,32]{0,2,1:T(8,128)(2,1)S(1)} %bitcast.111, bf16[7,384,10,32]{1,3,2,0:T(8,128)(2,1)} %get-tuple-element.231, s32[]{:T(128)} %get-tuple-element.220), kind=kOutput, calls=%fused_computation.3.clone.1 | convolution fusion | flops 230519040 | bytes 14941696 | tf_op jit(solution)/shard_map/while/body/eval_jaxpr/rhd,khd->hrk/dot_general | solution.py:60
  167.2 4.3 %fusion.60 = f32[10,384]{1,0:T(8,128)S(1)} fusion(f32[10,384,896]{2,1,0:T(8,128)S(1)} %get-tuple-element.190, f32[10,384]{1,0:T(8,128)S(1)} %broadcast_maximum_fusion.4, pred[384,896]{1,0:T(8,128)(4,1)S(1)} %get-tuple-element.230), kind=kLoop, calls=%fused_computation.4.clone.1 | loop fusion | flops 17199360 | bytes 14137344 | tf_op jit(solution)/shard_map/while/body/eval_jaxpr/reduce_sum | solution.py:66
  171.5 4.9 %fusion.61 = bf16[7,384,10,32]{1,3,2,0:T(8,128)(2,1)} fusion(bf16[7,384,10,32]{1,3,2,0:T(8,128)(2,1)} %get-tuple-element.221, s32[]{:T(128)} %get-tuple-element.220, bf16[896,10,32]{0,2,1:T(8,128)(2,1)S(1)} %bitcast.112, f32[10,384,896]{2,1,0:T(8,128)S(1)} %get-tuple-element.190, f32[10,384]{1,0:T(8,128)S(1)} %broadcast_maximum_fusion.4, ...), kind=kOutput, calls=%fused_computation.11.clone.1 | convolution fusion | flops 237527040 | bytes 15202816 | tf_op jit(solution)/shard_map/while/body/eval_jaxpr/hrk,khd->rhd/dot_general | solution.py:67
  176.4 1.3 constant_dynamic-slice_fusion.3
  177.7 3.8 %fusion.59 = (f32[10,384]{1,0:T(8,128)S(1)}, f32[10,384,896]{2,1,0:T(8,128)S(1)}) fusion(pred[384,896]{1,0:T(8,128)(4,1)S(1)} %get-tuple-element.230, bf16[896,10,32]{0,2,1:T(8,128)(2,1)S(1)} %bitcast.111, bf16[7,384,10,32]{1,3,2,0:T(8,128)(2,1)} %get-tuple-element.231, s32[]{:T(128)} %get-tuple-element.220), kind=kOutput, calls=%fused_computation.3.clone.1 | convolution fusion | flops 230519040 | bytes 14941696 | tf_op jit(solution)/shard_map/while/body/eval_jaxpr/rhd,khd->hrk/dot_general | solution.py:60
  181.5 4.3 %fusion.60 = f32[10,384]{1,0:T(8,128)S(1)} fusion(f32[10,384,896]{2,1,0:T(8,128)S(1)} %get-tuple-element.190, f32[10,384]{1,0:T(8,128)S(1)} %broadcast_maximum_fusion.4, pred[384,896]{1,0:T(8,128)(4,1)S(1)} %get-tuple-element.230), kind=kLoop, calls=%fused_computation.4.clone.1 | loop fusion | flops 17199360 | bytes 14137344 | tf_op jit(solution)/shard_map/while/body/eval_jaxpr/reduce_sum | solution.py:66
  185.8 4.9 %fusion.61 = bf16[7,384,10,32]{1,3,2,0:T(8,128)(2,1)} fusion(bf16[7,384,10,32]{1,3,2,0:T(8,128)(2,1)} %get-tuple-element.221, s32[]{:T(128)} %get-tuple-element.220, bf16[896,10,32]{0,2,1:T(8,128)(2,1)S(1)} %bitcast.112, f32[10,384,896]{2,1,0:T(8,128)S(1)} %get-tuple-element.190, f32[10,384]{1,0:T(8,128)S(1)} %broadcast_maximum_fusion.4, ...), kind=kOutput, calls=%fused_computation.11.clone.1 | convolution fusion | flops 237527040 | bytes 15202816 | tf_op jit(solution)/shard_map/while/body/eval_jaxpr/hrk,khd->rhd/dot_general | solution.py:67
  190.7 1.3 constant_dynamic-slice_fusion.3
  192.1 3.8 %fusion.59 = (f32[10,384]{1,0:T(8,128)S(1)}, f32[10,384,896]{2,1,0:T(8,128)S(1)}) fusion(pred[384,896]{1,0:T(8,128)(4,1)S(1)} %get-tuple-element.230, bf16[896,10,32]{0,2,1:T(8,128)(2,1)S(1)} %bitcast.111, bf16[7,384,10,32]{1,3,2,0:T(8,128)(2,1)} %get-tuple-element.231, s32[]{:T(128)} %get-tuple-element.220), kind=kOutput, calls=%fused_computation.3.clone.1 | convolution fusion | flops 230519040 | bytes 14941696 | tf_op jit(solution)/shard_map/while/body/eval_jaxpr/rhd,khd->hrk/dot_general | solution.py:60
  195.9 4.3 %fusion.60 = f32[10,384]{1,0:T(8,128)S(1)} fusion(f32[10,384,896]{2,1,0:T(8,128)S(1)} %get-tuple-element.190, f32[10,384]{1,0:T(8,128)S(1)} %broadcast_maximum_fusion.4, pred[384,896]{1,0:T(8,128)(4,1)S(1)} %get-tuple-element.230), kind=kLoop, calls=%fused_computation.4.clone.1 | loop fusion | flops 17199360 | bytes 14137344 | tf_op jit(solution)/shard_map/while/body/eval_jaxpr/reduce_sum | solution.py:66
  200.2 4.9 %fusion.61 = bf16[7,384,10,32]{1,3,2,0:T(8,128)(2,1)} fusion(bf16[7,384,10,32]{1,3,2,0:T(8,128)(2,1)} %get-tuple-element.221, s32[]{:T(128)} %get-tuple-element.220, bf16[896,10,32]{0,2,1:T(8,128)(2,1)S(1)} %bitcast.112, f32[10,384,896]{2,1,0:T(8,128)S(1)} %get-tuple-element.190, f32[10,384]{1,0:T(8,128)S(1)} %broadcast_maximum_fusion.4, ...), kind=kOutput, calls=%fused_computation.11.clone.1 | convolution fusion | flops 237527040 | bytes 15202816 | tf_op jit(solution)/shard_map/while/body/eval_jaxpr/hrk,khd->rhd/dot_general | solution.py:67
  205.1 12.2 %while.20 = (s32[]{:T(128)}, f32[70,1024]{1,0:T(8,128)S(1)}, s32[]{:T(128)}, bf16[16,70,1024]{2,1,0:T(8,128)(2,1)}, s32[]{:T(128)}, /*index=5*/s32[]{:T(128)}, s32[]{:T(128)}) while((s32[]{:T(128)}, f32[70,1024]{1,0:T(8,128)S(1)}, s32[]{:T(128)}, bf16[16,70,1024]{2,1,0:T(8,128)(2,1)}, s32[]{:T(128)}, /*index=5*/s32[]{:T(128)}, s32[]{:T(128)}) %tuple.70), condition=%wide.region_1.2_spmd, body=%wide.region_0.1_spmd.sunk | while | flops 143365 | bytes 716915 | solution.py:22
  205.1 1.0 convert_add_fusion.2
  208.2 1.0 convert_add_fusion.2
  217.6 1.0 copy.30
  218.6 2.1 fusion.27
  220.7 1.6 fusion.26
  (82 shorter events, 22.3 us)
Async XLA Ops:
  7.2 7.3 %copy-start = (bf16[384,2240]{0,1:T(8,128)(2,1)S(1)}, bf16[384,2240]{0,1:T(8,128)(2,1)}, u32[]{:S(2)}) copy-start(bf16[384,2240]{0,1:T(8,128)(2,1)} %param.19) | copy-start | bytes 5160964
  7.2 197.9 %all-gather.2.cloned.1.call-start = ((), (), s32[]{:S(2)}) async-start(), calls=%async_computation | async-start | bytes 2506752 | tf_op jit(solution)/shard_map/all_gather | solution.py:16
  7.2 30.6 %collective-permute-start = (bf16[1,128,2240]{1,2,0:T(8,128)(2,1)}, bf16[1,128,2240]{1,2,0:T(8,128)(2,1)}, u32[]{:S(2)}, u32[]{:S(2)}) collective-permute-start(bf16[1,128,2240]{1,2,0:T(8,128)(2,1)} %param.22), channel_id=1, source_target_pairs={{0,1},{1,2},{2,3},{3,4},{4,5},{5,6},{6,7},{7,8},{8,9},{9,10},{10,1... | collective-permute-start | bytes 1720328 | tf_op jit(solution)/shard_map/ppermute | solution.py:28
  9.3 30.4 %collective-permute-start.5 = (bf16[1,128,2240]{1,2,0:T(8,128)(2,1)}, bf16[1,128,2240]{1,2,0:T(8,128)(2,1)}, u32[]{:S(2)}, u32[]{:S(2)}) collective-permute-start(bf16[1,128,2240]{1,2,0:T(8,128)(2,1)} %param.21), channel_id=1, source_target_pairs={{0,1},{1,2},{2,3},{3,4},{4,5},{5,6},{6,7},{7,8},{8,9},{9,10},{10,1... | collective-permute-start | bytes 1720328 | tf_op jit(solution)/shard_map/ppermute | solution.py:28
  14.4 4.2 %copy-start.5 = (s32[16]{0:T(128)S(1)}, s32[16]{0:T(128)}, u32[]{:S(2)}) copy-start(s32[16]{0:T(128)} %param.25) | copy-start | bytes 196
  14.5 5.6 %copy-start.6 = (s32[16]{0:T(128)S(1)}, s32[16]{0:T(128)}, u32[]{:S(2)}) copy-start(s32[16]{0:T(128)} %param.27) | copy-start | bytes 196
  14.5 5.6 %copy-start.7 = (s32[16]{0:T(128)S(1)}, s32[16]{0:T(128)}, u32[]{:S(2)}) copy-start(s32[16]{0:T(128)} %param.26) | copy-start | bytes 196
  14.5 15.7 %copy-start.4 = (s32[16,3]{0,1:T(4,128)S(1)}, s32[16,3]{0,1:T(4,128)}, u32[]{:S(2)}) copy-start(s32[16,3]{0,1:T(4,128)} %param.28) | copy-start | bytes 580
  18.6 18.2 %copy-start.3 = (bf16[1,128,2240]{1,2,0:T(8,128)(2,1)S(1)}, bf16[1,128,2240]{1,2,0:T(8,128)(2,1)}, u32[]{:S(2)}) copy-start(bf16[1,128,2240]{1,2,0:T(8,128)(2,1)} %param.21) | copy-start | bytes 1720324
  18.7 23.0 %copy-start.2 = (bf16[384,2240]{0,1:T(8,128)(2,1)S(1)}, bf16[384,2240]{0,1:T(8,128)(2,1)}, u32[]{:S(2)}) copy-start(bf16[384,2240]{0,1:T(8,128)(2,1)} %param.17) | copy-start | bytes 5160964
  37.8 18.6 %collective-permute-start.1 = (bf16[1,128,2240]{1,2,0:T(8,128)(2,1)}, bf16[1,128,2240]{1,2,0:T(8,128)(2,1)}, u32[]{:S(2)}, u32[]{:S(2)}) collective-permute-start(bf16[1,128,2240]{1,2,0:T(8,128)(2,1)} %collective-permute-done), channel_id=1, source_target_pairs={{0,1},{1,2},{2,3},{3,4},{4,5},{5,6},{6,7},{7,8},{8,9},{9,10},{10,1... | collective-permute-start | bytes 1720328 | tf_op jit(solution)/shard_map/ppermute | solution.py:28
  39.7 25.9 %collective-permute-start.6 = (bf16[1,128,2240]{1,2,0:T(8,128)(2,1)}, bf16[1,128,2240]{1,2,0:T(8,128)(2,1)}, u32[]{:S(2)}, u32[]{:S(2)}) collective-permute-start(bf16[1,128,2240]{1,2,0:T(8,128)(2,1)} %collective-permute-done.5), channel_id=1, source_target_pairs={{0,1},{1,2},{2,3},{3,4},{4,5},{5,6},{6,7},{7,8},{8,9},{9,10},{10,1... | collective-permute-start | bytes 1720328 | tf_op jit(solution)/shard_map/ppermute | solution.py:28
  56.3 15.4 %collective-permute-start.2 = (bf16[1,128,2240]{1,2,0:T(8,128)(2,1)}, bf16[1,128,2240]{1,2,0:T(8,128)(2,1)}, u32[]{:S(2)}, u32[]{:S(2)}) collective-permute-start(bf16[1,128,2240]{1,2,0:T(8,128)(2,1)} %collective-permute-done.1), channel_id=1, source_target_pairs={{0,1},{1,2},{2,3},{3,4},{4,5},{5,6},{6,7},{7,8},{8,9},{9,10},{10,1... | collective-permute-start | bytes 1720328 | tf_op jit(solution)/shard_map/ppermute | solution.py:28
  65.6 12.3 %collective-permute-start.7 = (bf16[1,128,2240]{1,2,0:T(8,128)(2,1)}, bf16[1,128,2240]{1,2,0:T(8,128)(2,1)}, u32[]{:S(2)}, u32[]{:S(2)}) collective-permute-start(bf16[1,128,2240]{1,2,0:T(8,128)(2,1)} %collective-permute-done.6), channel_id=1, source_target_pairs={{0,1},{1,2},{2,3},{3,4},{4,5},{5,6},{6,7},{7,8},{8,9},{9,10},{10,1... | collective-permute-start | bytes 1720328 | tf_op jit(solution)/shard_map/ppermute | solution.py:28
  71.8 14.0 %collective-permute-start.3 = (bf16[1,128,2240]{1,2,0:T(8,128)(2,1)}, bf16[1,128,2240]{1,2,0:T(8,128)(2,1)S(1)}, u32[]{:S(2)}, u32[]{:S(2)}) collective-permute-start(bf16[1,128,2240]{1,2,0:T(8,128)(2,1)} %collective-permute-done.2), channel_id=1, source_target_pairs={{0,1},{1,2},{2,3},{3,4},{4,5},{5,6},{6,7},{7,8},{8,9},{9,10},{10,1... | collective-permute-start | bytes 1720328 | tf_op jit(solution)/shard_map/ppermute | solution.py:28
  77.9 12.2 %collective-permute-start.8 = (bf16[1,128,2240]{1,2,0:T(8,128)(2,1)}, bf16[1,128,2240]{1,2,0:T(8,128)(2,1)S(1)}, u32[]{:S(2)}, u32[]{:S(2)}) collective-permute-start(bf16[1,128,2240]{1,2,0:T(8,128)(2,1)} %collective-permute-done.7), channel_id=1, source_target_pairs={{0,1},{1,2},{2,3},{3,4},{4,5},{5,6},{6,7},{7,8},{8,9},{9,10},{10,1... | collective-permute-start | bytes 1720328 | tf_op jit(solution)/shard_map/ppermute | solution.py:28
  85.8 12.0 %collective-permute-start.4 = (bf16[1,128,2240]{1,2,0:T(8,128)(2,1)S(1)}, bf16[1,128,2240]{1,2,0:T(8,128)(2,1)S(1)}, u32[]{:S(2)}, u32[]{:S(2)}) collective-permute-start(bf16[1,128,2240]{1,2,0:T(8,128)(2,1)S(1)} %collective-permute-done.3), channel_id=1, source_target_pairs={{0,1},{1,2},{2,3},{3,4},{4,5},{5,6},{6,7},{7,8},{8,9},{9,10},{10,1... | collective-permute-start | bytes 1720328 | tf_op jit(solution)/shard_map/ppermute | solution.py:28
  90.1 13.7 %collective-permute-start.9 = (bf16[1,128,2240]{1,2,0:T(8,128)(2,1)S(1)}, bf16[1,128,2240]{1,2,0:T(8,128)(2,1)S(1)}, u32[]{:S(2)}, u32[]{:S(2)}) collective-permute-start(bf16[1,128,2240]{1,2,0:T(8,128)(2,1)S(1)} %collective-permute-done.8), channel_id=1, source_target_pairs={{0,1},{1,2},{2,3},{3,4},{4,5},{5,6},{6,7},{7,8},{8,9},{9,10},{10,1... | collective-permute-start | bytes 1720328 | tf_op jit(solution)/shard_map/ppermute | solution.py:28
  205.1 12.4 %copy-start.1 = (f32[70,32,32]{0,2,1:T(8,128)S(1)}, f32[70,32,32]{0,2,1:T(8,128)}, u32[]{:S(2)}) copy-start(f32[70,32,32]{0,2,1:T(8,128)} %copy.29) | copy-start | bytes 860164
  217.5 3.2 %copy-start.8 = (f32[2240]{0:T(1024)S(1)}, f32[2240]{0:T(1024)}, u32[]{:S(2)}) copy-start(f32[2240]{0:T(1024)} %param.29) | copy-start | bytes 26884
Sparse Core Ops, SparseCore 0:
  18.7 43.7 all-gather.1
where the time goes:
time: 231 us; the launch traced here: 229 us
  matrix products  64.5 us (28%)
  other arithmetic  51 us (22%)
  local copies, waits for them, and re-layouts  38.6 us (17%)
  waiting for transfers between devices  31.8 us (14%)
  between operations  22 us (10%)
  starting transfers between devices  20.9 us (9%)
    dot_general x7, matrix products, attend_block(): jnp.einsum('hrk,khd->rhd', expo.astype(jnp.bfloat16), values_three, prefe...  34.4 us
    ppermute x10, waiting for transfers between devices, passed_along(): return lax.ppermute(block, axis, route)  31.7 us
    reduce_sum x7, other arithmetic, attend_block(): run_sum = jnp.sum(expo, axis=2)  30 us
    dot_general x7, matrix products, attend_block(): jnp.einsum('rhd,khd->hrk', query_rows, keys_three, preferred_element_type...  26.5 us
    ppermute x10, starting transfers between devices, passed_along(): return lax.ppermute(block, axis, route)  20.9 us
    unnamed x36, local copies, waits for them, and re-layouts  20.6 us
    add x12, other arithmetic, add_states(): return earlier + later  11.9 us
    dynamic_slice x7, local copies, waits for them, and re-layouts, joined_attention(): mixed_groups = lax.map(one_group, (query_groups, key_groups, value_groups))  9.27 us
  transfers between devices with their start and end apart: 11, of which 6 were waited for; matrix products, arithmetic and copies ran while one was open for 60% of the time, Pallas kernels for 0%

commit v1 on v0

v1 whole, which is shorter than its diff:
```python
import functools
import math

import jax
import jax.numpy as jnp
from jax import lax
from jax.experimental import pallas as pl
from jax.experimental.pallas import tpu as pltpu
from jax.sharding import PartitionSpec as P

HD = 32
SPAN = 6
QUAD = 128
LAYER = 4
BF = jnp.bfloat16
F32 = jnp.float32
EMPTY = -1e30
STEP = 3
PARTS = 3
COPIES = 2
ROOM = 66_400_000


def vmem():
    return pl.BlockSpec(memory_space=pltpu.VMEM)


def smem():
    return pl.BlockSpec(memory_space=pltpu.SMEM)


def anywhere():
    return pl.BlockSpec(memory_space=pl.ANY)


def cost(flops, moved, exps=0):
    flops, moved = flops // 1000, moved // 1000
    return pl.CostEstimate(flops=flops, bytes_accessed=moved, transcendentals=exps)


def quad_rows(ref, q, width):
    if (q + 1) * QUAD <= width:
        return ref[q * QUAD : (q + 1) * QUAD, :]
    part = ref[q * QUAD : width, :]
    fill = jnp.zeros(((q + 1) * QUAD - width, part.shape[1]), part.dtype)
    return jnp.concatenate([part, fill], axis=0)


def part_rows(width, quads, part):
    low = part * (quads // PARTS) * QUAD
    return pl.ds(low, min(quads // PARTS * QUAD, width - low))


def turned_quad(keys, used, rows):
    turned = jnp.transpose(keys.astype(F32))
    return jnp.where(rows < used, turned, turned[0:1, :]).astype(BF)


def turn_kernel(tokens_ref, keys_hbm, out_hbm, keys, out, in_sems, out_sems):
    used = tokens_ref[lax.axis_index("tm")]
    width, quads = keys.shape[0], out.shape[0]
    every = quads // PARTS
    rows = lax.broadcasted_iota(jnp.int32, (QUAD, QUAD), 0)

    def move_in(part):
        at = part_rows(width, quads, part)
        return pltpu.make_async_copy(keys_hbm.at[at], keys.at[at], in_sems.at[part])

    def move_out(part):
        at = pl.ds(part * every, every)
        return pltpu.make_async_copy(out.at[at], out_hbm.at[at], out_sems.at[part])

    for part in range(PARTS):
        move_in(part).start()
    for q in range(quads):
        if q % every == 0:
            move_in(q // every).wait()
        out[q] = turned_quad(quad_rows(keys, q, width), used, rows)
        if q % every == every - 1:
            move_out(q // every).start()
    for part in range(PARTS):
        move_out(part).wait()


def turned_keys(tokens, keys):
    width, slots = keys.shape
    shape = (-(-width // QUAD), slots, QUAD)
    return pl.pallas_call(
        turn_kernel,
        in_specs=[smem(), anywhere()],
        out_specs=anywhere(),
        out_shape=jax.ShapeDtypeStruct(shape, BF),
        scratch_shapes=[
            pltpu.VMEM((width, slots), BF),
            pltpu.VMEM(shape, BF),
            pltpu.SemaphoreType.DMA((PARTS,)),
            pltpu.SemaphoreType.DMA((PARTS,)),
        ],
        cost_estimate=cost(0, 4 * width * slots),
        compiler_params=pltpu.CompilerParams(vmem_limit_bytes=ROOM),
        name="turned_keys",
    )(tokens, keys)


def no_kernel(*refs):
    del refs


def after(blocks, *tokens):
    return pl.pallas_call(
        no_kernel,
        in_specs=[anywhere()] * (len(blocks) + len(tokens)),
        out_specs=[anywhere()] * len(blocks),
        out_shape=[jax.ShapeDtypeStruct(block.shape, block.dtype) for block in blocks],
        input_output_aliases={place: place for place in range(len(blocks))},
        cost_estimate=cost(0, 0),
        name="after",
    )(*blocks, *tokens)


def across_kernel(waits, own_hbm, up_hbm, *refs):
    *refs, held, in_sems, out_sems = refs[waits:]
    summed = len(refs) > 2
    if summed:
        *states, across_hbm, _, sent_out = refs
    else:
        across_hbm, _ = refs
    lower = lax.axis_index("tm") % LAYER < LAYER // 2
    piece = own_hbm.shape[0] // COPIES

    def move_in(source, part):
        at = pl.ds(part * piece, piece)
        return pltpu.make_async_copy(source.at[at], held.at[at], in_sems.at[part])

    def move_out(part):
        at = pl.ds(part * piece, piece)
        return pltpu.make_async_copy(held.at[at], across_hbm.at[at], out_sems.at[part])

    @pl.when(lower)
    def _():
        for part in range(COPIES):
            move_in(own_hbm, part).start()

    @pl.when(jnp.logical_not(lower))
    def _():
        for part in range(COPIES):
            move_in(up_hbm, part).start()

    if summed:
        digit_step(states[0], states[1:], sent_out)
    for part in range(COPIES):
        move_in(up_hbm, part).wait()
        move_out(part).start()
    for part in range(COPIES):
        move_out(part).wait()


def to_cross(own, up, *tokens, states=()):
    shape = jax.ShapeDtypeStruct(own.shape, own.dtype)
    outs, out_specs = [shape, shape], [anywhere()] * 2
    if states:
        outs.append(jax.ShapeDtypeStruct(states[0].shape, BF))
        out_specs.append(vmem())
    return pl.pallas_call(
        functools.partial(across_kernel, len(tokens)),
        in_specs=[anywhere()] * (2 + len(tokens)) + [vmem()] * len(states),
        out_specs=out_specs,
        out_shape=outs,
        input_output_aliases={1: 1},
        scratch_shapes=[
            pltpu.VMEM(own.shape, own.dtype),
            pltpu.SemaphoreType.DMA((COPIES,)),
            pltpu.SemaphoreType.DMA((COPIES,)),
        ],
        cost_estimate=cost(0, 4 * own.size),
        compiler_params=pltpu.CompilerParams(vmem_limit_bytes=ROOM),
        name="to_cross",
    )(own, up, *tokens, *states)


def attend_kernel(setup, start_ref, end_ref, tokens_ref, region_ref, *refs):
    count, first, last, held, waits, prompts, width, tokens, tiles = setup
    tile = tokens // tiles
    quads = -(-width // QUAD)
    rounds = quads // STEP
    every = quads // PARTS
    query_refs, refs = refs[:PARTS], refs[PARTS:]
    if first:
        raw_keys, refs = refs[0], refs[1:]
    key_hbm = [None] * first + list(refs[: count - first])
    refs = refs[count - first :]
    value_hbm, refs = refs[:count], refs[count + waits :]
    if not first:
        level_in, total_in = refs[0], refs[1 : 1 + PARTS]
        refs = refs[1 + PARTS :]
    if last:
        out_ref, refs = refs[0], refs[1:]
    else:
        level_out, total_out = refs[0], refs[1 : 1 + PARTS]
        refs = refs[1 + PARTS :]
    keys, vals, marks, spread, level, total, s_a, s_b, p_a, p_b, f_a, f_b, work, found, used, ready, sems = refs
    scale = math.log2(math.e) / math.sqrt(HD)
    none = jnp.zeros((HD, tile), BF)
    i = pl.program_id(0)

    def copies(b):
        moves = [pltpu.make_async_copy(value_hbm[b], vals.at[b, pl.ds(0, width)], sems.at[b, 1])]
        if key_hbm[b] is not None:
            moves.append(pltpu.make_async_copy(key_hbm[b], keys.at[b], sems.at[b, 0]))
        return moves

    @pl.when(i == 0)
    def _():
        stretch = lax.axis_index("tm")
        wanted = []
        lengths = [jnp.int32(0)] * tiles
        for b, owner in enumerate(held(stretch)):
            if owner is None:
                seen = [jnp.int32(1)] * tiles
                used[b] = jnp.int32(QUAD)
            else:
                safe = jnp.clip(owner, 0, prompts - 1)
                covers = (
                    (owner >= 0)
                    & (start_ref[safe] <= stretch)
                    & (stretch < end_ref[safe])
                )
                used[b] = tokens_ref[safe]
                seen = [
                    (covers & (region_ref[t, safe] == 1)).astype(jnp.int32)
                    for t in range(tiles)
                ]
            for t in range(tiles):
                work[t * count + lengths[t]] = jnp.int32(b)
                lengths[t] = lengths[t] + seen[t]
            wanted.append(functools.reduce(jnp.add, seen) > 0)
            ready[b] = jnp.int32(0)

            @pl.when(wanted[b])
            def _():
                for move in copies(b):
                    move.start()

        for t in range(tiles):
            found[t] = lengths[t]
        for q in range(quads):
            for h in range(QUAD // HD):
                off = (1 - h % 2) * tile
                spread[q, h * HD : (h + 1) * HD, off : off + tile] = none
        lanes = lax.broadcasted_iota(jnp.int32, (16, QUAD), 1)
        rows = lax.broadcasted_iota(jnp.int32, (QUAD, QUAD), 0)
        for b in range(count):
            marks[b] = jnp.where(lanes < used[b], 1.0, 0.0).astype(BF)
            if width < quads * QUAD:
                vals[b, width:, :] = jnp.zeros((quads * QUAD - width, QUAD), BF)
            if key_hbm[b] is None:
                for q in range(quads):
                    keys[b, q] = turned_quad(quad_rows(raw_keys, q, width), QUAD, rows)

    def arrived(b):
        @pl.when(ready[b] == 0)
        def _():
            pltpu.make_async_copy(value_hbm[-1], vals.at[b, pl.ds(0, width)], sems.at[b, 1]).wait()
            ready[b] = jnp.int32(1)
            if key_hbm[-1] is None:
                return

            @pl.when(b >= first)
            def _():
                pltpu.make_async_copy(key_hbm[-1], keys.at[b], sems.at[b, 0]).wait()

    low_half = lax.broadcasted_iota(jnp.int32, (QUAD, QUAD), 1) < QUAD // 2
    row16 = lax.broadcasted_iota(jnp.int32, (16, QUAD), 0)
    zeros = jnp.zeros((QUAD // 2, QUAD), BF)

    def score(b, g, s_to):
        for k in range(STEP):
            block = keys[b, g * STEP + k].astype(F32)
            both = jnp.concatenate(
                [jnp.where(low_half, block, 0.0), jnp.where(low_half, 0.0, block)], axis=0
            ).astype(BF)
            s_to[k] = jnp.dot(both, spread[g * STEP + k], preferred_element_type=F32)

    def weigh(g, s_from, p_to, f_to):
        for k in range(STEP):
            q = g * STEP + k
            for pair in range(2):
                at = slice(pair * QUAD, (pair + 1) * QUAD)
                part = s_from[k, at, :]
                old = level[q, pair : pair + 1]
                new = jnp.maximum(old, jnp.max(part, axis=0, keepdims=True))
                p_to[k, at, :] = jnp.exp2((part - new) * scale).astype(BF)
                f_to[k, pair : pair + 1] = jnp.exp2((old - new) * scale)
                level[q, pair : pair + 1] = new

    def mix(b, many, ones, g, p_from, f_from):
        for k in range(STEP):
            q = g * STEP + k
            v = vals[b, q * QUAD : (q + 1) * QUAD, :] * many
            left = jnp.concatenate(
                [
                    jnp.concatenate([v[: QUAD // 2], zeros], axis=1),
                    jnp.concatenate([zeros, v[QUAD // 2 :]], axis=1),
                    ones,
                ],
                axis=0,
            )
            out = jnp.dot(left, p_from[k], preferred_element_type=F32)
            factor = f_from[k]
            level[q, 2:4] = level[q, 2:4] * factor + out[QUAD : QUAD + 2]
            for pair in range(2):
                r = pair * 2 * HD
                added = jnp.concatenate([out[r : r + HD, :tile], out[r + HD : r + 2 * HD, tile:]], axis=1)
                at = slice(pair * HD, (pair + 1) * HD)
                total[q, at, :] = total[q, at, :] * factor[pair : pair + 1] + added

    slots = [(s_a, p_a, f_a), (s_b, p_b, f_b)]
    n = found[i]
    if first:
        level[:, 0:2] = jnp.full((quads, 2, 2 * tile), EMPTY, F32)
        level[:, 2:4] = jnp.zeros((quads, 2, 2 * tile), F32)
        total[...] = jnp.zeros(total.shape, F32)
    else:
        level[...] = level_in[0]
        for part in range(PARTS):
            total[part * every : (part + 1) * every] = total_in[part][0]

    @pl.when(n > 0)
    def _():
        for r in range(0, quads * QUAD, HD):
            q, h = r // QUAD, r % QUAD // HD
            on = h % 2 * tile
            low = q // every * every * QUAD
            piece = query_refs[q // every][r - low : r - low + HD, :] if r < width else none
            spread[q, h * HD : (h + 1) * HD, on : on + tile] = piece
        b0 = work[i * count]
        arrived(b0)
        score(b0, 0, s_a)
        weigh(0, s_a, p_a, f_a)
        score(b0, 1, s_b)

        def entry(j, carry):
            b = work[i * count + j]
            later = work[i * count + jnp.minimum(j + 1, n - 1)]
            arrived(later)
            mark = marks[b]
            many = jnp.concatenate([mark] * (QUAD // 16), axis=0)
            mark = mark.astype(F32)
            ones = jnp.concatenate(
                [jnp.where(row16 == 0, mark, 0.0), jnp.where(row16 == 1, mark, 0.0)], axis=1
            ).astype(BF)
            for g in range(rounds):
                here, there = slots[g % 2], slots[(g + 1) % 2]
                score(b if g + 2 < rounds else later, (g + 2) % rounds, here[0])
                mix(b, many, ones, g, here[1], here[2])
                weigh((g + 1) % rounds, there[0], there[1], there[2])
            return carry

        lax.fori_loop(0, n, entry, 0)

    if last:
        for q in range(quads):
            scaled = 1.0 / level[q, 2:4]
            for pair in range(2):
                mixed = total[q, pair * HD : (pair + 1) * HD, :] * scaled[pair : pair + 1]
                for side in range(2):
                    r = q * QUAD + (2 * pair + side) * HD
                    if r < width:
                        out_ref[r : r + HD, :] = mixed[:, side * tile : (side + 1) * tile].astype(BF)
    else:
        level_out[0] = level[...]
        for part in range(PARTS):
            total_out[part][0] = total[part * every : (part + 1) * every]


def attend(spans, queries, blocks, held, state, last, waits=()):
    width, tokens = queries.shape
    quads = -(-width // QUAD)
    every = quads // PARTS
    count = len(blocks)
    tiles, prompts = spans[3].shape
    tile = tokens // tiles
    first = state is None
    setup = (count, int(first), last, held, len(waits), prompts, width, tokens, tiles)
    levels, totals = (quads, 4, 2 * tile), (every, 2 * HD, 2 * tile)
    state_shapes = [(tiles,) + shape for shape in (levels,) + (totals,) * PARTS]
    state_specs = [pl.BlockSpec((1,) + shape[1:], lambda i: (i, 0, 0, 0)) for shape in state_shapes]
    query_specs = [pl.BlockSpec((every * QUAD, tile), lambda i, p=p: (p, i)) for p in range(PARTS)]
    if last:
        outs = [jax.ShapeDtypeStruct((width, tokens), BF)]
        out_specs = [pl.BlockSpec((width, tile), lambda i: (0, i))]
    else:
        outs = [jax.ShapeDtypeStruct(shape, F32) for shape in state_shapes]
        out_specs = list(state_specs)
    raw = [blocks[0][0]] if first else []
    keys = [block[0] for block in blocks[int(first) :]]
    values = [block[1] for block in blocks]
    scratch = [
        pltpu.VMEM((count, quads, QUAD, QUAD), BF),
        pltpu.VMEM((count, quads * QUAD, QUAD), BF),
        pltpu.VMEM((count, 16, QUAD), BF),
        pltpu.VMEM((quads, QUAD, 2 * tile), BF),
        pltpu.VMEM(levels, F32),
        pltpu.VMEM((quads, 2 * HD, 2 * tile), F32),
    ]
    scratch += [pltpu.VMEM((STEP, 2 * QUAD, 2 * tile), F32)] * 2
    scratch += [pltpu.VMEM((STEP, 2 * QUAD, 2 * tile), BF)] * 2
    scratch += [pltpu.VMEM((STEP, 2, 2 * tile), F32)] * 2
    scratch += [
        pltpu.SMEM((count * tiles + 1,), jnp.int32),
        pltpu.SMEM((tiles,), jnp.int32),
        pltpu.SMEM((count,), jnp.int32),
        pltpu.SMEM((count,), jnp.int32),
        pltpu.SemaphoreType.DMA((count, 2)),
    ]
    area = count * QUAD * tokens
    return pl.pallas_call(
        functools.partial(attend_kernel, setup),
        grid=(tiles,),
        in_specs=[smem()] * 4
        + query_specs
        + [pl.BlockSpec(a.shape, lambda i: (0, 0)) for a in raw]
        + [anywhere()] * (len(keys) + len(values) + len(waits))
        + state_specs * (not first),
        out_specs=out_specs,
        out_shape=outs,
        scratch_shapes=scratch,
        cost_estimate=cost(40 * area * width, 4 * width * tokens, area * width // HD),
        compiler_params=pltpu.CompilerParams(vmem_limit_bytes=ROOM),
        name="attend",
    )(
        *spans,
        *[queries] * PARTS,
        *raw,
        *keys,
        *values,
        *waits,
        *([] if first else state),
    )


def state_kernel(keys_hbm, values_hbm, own_ref, sent_ref, keys, values, sems):
    rows = lax.broadcasted_iota(jnp.int32, (QUAD, QUAD), 0) // HD
    columns = lax.broadcasted_iota(jnp.int32, (QUAD, QUAD), 1) // HD
    width, quads = keys.shape[0], sent_ref.shape[0]

    def moves(part):
        at = part_rows(width, quads, part)
        return (
            pltpu.make_async_copy(keys_hbm.at[at], keys.at[at], sems.at[2 * part]),
            pltpu.make_async_copy(values_hbm.at[at], values.at[at], sems.at[2 * part + 1]),
        )

    for part in range(PARTS):
        for move in moves(part):
            move.start()
    for q in range(quads):
        if q % (quads // PARTS) == 0:
            for move in moves(q // (quads // PARTS)):
                move.wait()
        lifted = jnp.maximum(quad_rows(keys, q, width), 0)
        grown = lax.dot_general(
            quad_rows(values, q, width), lifted, (((1,), (1,)), ((), ())), preferred_element_type=F32
        )
        grown = jnp.where(rows == columns, grown, 0.0)
        folded = grown[0:HD] + grown[HD : 2 * HD] + grown[2 * HD : 3 * HD] + grown[3 * HD :]
        own_ref[q] = folded
        sent_ref[q] = folded.astype(BF)


def stretch_states(keys, values):
    width, tokens = keys.shape
    quads = -(-width // QUAD)
    shape = (quads, HD, QUAD)
    return pl.pallas_call(
        state_kernel,
        in_specs=[anywhere()] * 2,
        out_specs=[vmem()] * 2,
        out_shape=[jax.ShapeDtypeStruct(shape, F32), jax.ShapeDtypeStruct(shape, BF)],
        scratch_shapes=[
            pltpu.VMEM((width, tokens), BF),
            pltpu.VMEM((width, tokens), BF),
            pltpu.SemaphoreType.DMA((2 * PARTS,)),
        ],
        cost_estimate=cost(8 * width * QUAD * tokens, 4 * width * tokens),
        compiler_params=pltpu.CompilerParams(vmem_limit_bytes=ROOM),
        name="stretch_states",
    )(keys, values)


def lower_sum(hop, prior, partners):
    digit = lax.axis_index("tm") // hop % (len(partners) + 1)
    for d, partner in enumerate(partners, 1):
        prior = prior + jnp.where((digit ^ d) < digit, partner.astype(F32), 0.0)
    return prior


def digit_step(own_ref, partners, sent_out):
    for q in range(sent_out.shape[0]):
        whole = own_ref[q]
        for partner in partners:
            whole = whole + partner[q].astype(F32)
        sent_out[q] = whole.astype(BF)


def digit_kernel(own_ref, *refs):
    digit_step(own_ref, refs[:-2], refs[-1])


def digit_sums(own, partners, token):
    return pl.pallas_call(
        digit_kernel,
        in_specs=[vmem()] * (1 + len(partners)) + [anywhere()],
        out_specs=vmem(),
        out_shape=jax.ShapeDtypeStruct(own.shape, BF),
        cost_estimate=cost(0, 8 * own.size),
        compiler_params=pltpu.CompilerParams(vmem_limit_bytes=ROOM),
        name="digit_sums",
    )(own, *partners, token)


def digits_of(size):
    hop, digits = 1, []
    while hop < size:
        radix = 4 if size // hop % 4 == 0 else 2
        digits.append((hop, radix))
        hop *= radix
    return digits


def swapped(block, hop, radix):
    size = lax.axis_size("tm")
    return [sent(block, [(i, i ^ (d * hop)) for i in range(size)]) for d in range(1, radix)]


def norm_kernel(digits, queries_hbm, own_ref, gain_ref, *refs):
    partners, refs = refs[:-7], refs[-6:]
    out_hbm, queries, raw, out, in_sems, out_sems = refs
    rows = lax.broadcasted_iota(jnp.int32, (QUAD, QUAD), 0) // HD
    columns = lax.broadcasted_iota(jnp.int32, (QUAD, QUAD), 1) // HD
    width = queries.shape[0]
    quads, tokens = raw.shape[0], raw.shape[2]
    every = quads // PARTS

    def move_in(part):
        at = part_rows(width, quads, part)
        return pltpu.make_async_copy(queries_hbm.at[at], queries.at[at], in_sems.at[part])

    def move_out(part):
        at = part_rows(width, quads, part)
        return pltpu.make_async_copy(out.at[at], out_hbm.at[at], out_sems.at[part])

    for part in range(PARTS):
        move_in(part).start()
    squares = jnp.zeros((1, tokens), F32)
    for q in range(quads):
        if q % every == 0:
            move_in(q // every).wait()
        whole, rest = own_ref[q], partners
        for hop, radix in digits:
            whole = lower_sum(hop, whole, [partner[q] for partner in rest[: radix - 1]])
            rest = rest[radix - 1 :]
        whole = whole.astype(BF).astype(F32)
        wide = jnp.where(rows == columns, jnp.concatenate([whole] * (QUAD // HD), axis=0), 0.0).astype(BF)
        lifted = jnp.maximum(quad_rows(queries, q, width), 0)
        part = jnp.dot(wide, lifted, preferred_element_type=F32)
        raw[q] = part
        squares = squares + jnp.sum(part * part, axis=0, keepdims=True)
    factor = lax.rsqrt(squares / width + 1e-05)
    for q in range(quads):
        size = min(QUAD, width - q * QUAD)
        gains = jnp.transpose(jnp.broadcast_to(gain_ref[q : q + 1, :], (QUAD, QUAD)))
        gains = jnp.concatenate([gains] * (tokens // QUAD), axis=1)
        mixed = (raw[q] * factor * gains).astype(BF)
        out[q * QUAD : q * QUAD + size, :] = mixed[:size]
        if q % every == every - 1:
            move_out(q // every).start()
    for part in range(PARTS):
        move_out(part).wait()


def self_mix(queries, own, gain, partners, digits, token):
    width, tokens = queries.shape
    quads = -(-width // QUAD)
    return pl.pallas_call(
        functools.partial(norm_kernel, tuple(digits)),
        in_specs=[anywhere()] + [vmem()] * (2 + len(partners)) + [anywhere()],
        out_specs=anywhere(),
        out_shape=jax.ShapeDtypeStruct((width, tokens), BF),
        scratch_shapes=[
            pltpu.VMEM((width, tokens), BF),
            pltpu.VMEM((quads, QUAD, tokens), F32),
            pltpu.VMEM((width, tokens), BF),
            pltpu.SemaphoreType.DMA((PARTS,)),
            pltpu.SemaphoreType.DMA((PARTS,)),
        ],
        cost_estimate=cost(8 * width * QUAD * tokens, 4 * width * tokens),
        compiler_params=pltpu.CompilerParams(vmem_limit_bytes=ROOM),
        name="self_mix",
    )(queries, own, jnp.pad(gain, (0, quads * QUAD - width)).reshape(quads, QUAD), *partners, token)


def sent(block, pairs):
    return lax.ppermute(block, "tm", pairs)


def local(
    queries,
    keys,
    values,
    cross_queries,
    prompt_keys,
    prompt_values,
    caption_keys,
    caption_values,
    span_start,
    span_end,
    prompt_tokens,
    region_mask,
    out_gain,
):
    size = lax.axis_size("tm")
    slots, width = prompt_keys.shape[1:]
    spans = (span_start, span_end, prompt_tokens, jnp.transpose(region_mask))
    turned = lambda block: jnp.transpose(block.reshape(slots, width))
    queries_t = jnp.transpose(cross_queries)
    call = functools.partial(attend, spans, queries_t)

    bases = [LAYER * z for z in range(size // LAYER)]
    beside = [(i, i ^ 1) for i in range(size)]
    up = [(i, (i + LAYER) % size) for i in range(size)]
    swap = [(i, i ^ 2) for i in range(size)]
    onward = [(i, i + LAYER - 1) for i in range(size) if i % 2 and i + LAYER - 1 < size]
    further = [(i, i + 1) for i in range(size) if i % 2 and i + 1 < size]
    spot = lambda c: c % LAYER
    pick = lambda c, *ways: functools.reduce(
        lambda rest, way: jnp.where(spot(c) == way[0], c - way[1], rest), ways, -1
    )
    digits = digits_of(size)

    own_v = turned(prompt_values)
    up_v = sent(own_v, up)
    own_k = turned_keys(prompt_tokens, turned(prompt_keys))
    own_sums, going = stretch_states(jnp.transpose(keys), jnp.transpose(values))
    caption = (jnp.transpose(caption_keys), jnp.transpose(caption_values))
    state = call([caption], lambda c: [None], None, False, waits=[own_k, going])

    partners = swapped(going, *digits[0])
    own_v_beside = sent(own_v, beside)
    own_k_beside = sent(own_k, beside)
    across_v, up_v, going = to_cross(
        own_v, up_v, state[0], own_v_beside, own_k_beside, states=[own_sums, *partners]
    )
    swap_v = sent(across_v, swap)
    (late_k,) = after([own_k], state[0], own_k_beside)
    up_k = sent(late_k, up)
    up_v_beside = sent(up_v, beside)
    for digit in digits[1:-1]:
        partners += swapped(going, *digit)
        going = digit_sums(own_sums, partners, state[0])
    final = swapped(going, *digits[-1]) if len(digits) > 1 else []
    state = call([(late_k, own_v)], lambda c: [c], state, False, waits=[across_v])

    swap_v, up_v_beside = after([swap_v, up_v_beside], state[0])
    across_k, up_k = to_cross(late_k, up_k, state[0], swap_v, up_v_beside, *final[:2])
    swap_k = sent(across_k, swap)
    far_k = sent(up_k, further)
    far_v = sent(swap_v, onward)
    up_k_beside = sent(up_k, beside)
    state = call(
        [(own_k_beside, own_v_beside), (up_k, up_v), (up_k_beside, up_v_beside)],
        lambda c: [
            pick(c, (1, 1), (3, 1)),
            c - LAYER,
            pick(c, (0, 3), (2, 3), (1, 5), (3, 5)),
        ],
        state,
        False,
        waits=[across_k],
    )

    self_mixed = self_mix(jnp.transpose(queries), own_sums, out_gain, partners + final, digits, state[0])
    swap_k, swap_v = after([swap_k, swap_v], state[0], self_mixed, far_k, far_v)
    swap_v_beside = sent(swap_v, beside)
    swap_k_beside = sent(swap_k, beside)
    cross_mixed = call(
        [(swap_k, swap_v), (swap_k_beside, swap_v_beside), (far_k, far_v)],
        lambda c: [
            c - 2,
            pick(c, (0, 1), (1, 3), (2, 1), (3, 3)),
            pick(c, (0, 5), (2, 5)),
        ],
        state,
        True,
    )[0]
    return (jnp.transpose(self_mixed), jnp.transpose(cross_mixed))


def solution(mesh):
    in_specs = (
        P(("groups", "tm"), None),
        P(("groups", "tm"), None),
        P(("groups", "tm"), None),
        P(("groups", "tm"), None),
        P(("groups", "tm"), None, None),
        P(("groups", "tm"), None, None),
        P("groups", None),
        P("groups", None),
        P("groups"),
        P("groups"),
        P("groups"),
        P("groups", None),
        P(),
    )
    out_specs = (P(("groups", "tm"), None), P(("groups", "tm"), None))
    return jax.shard_map(local, mesh=mesh, in_specs=in_specs, out_specs=out_specs, check_vma=False)
```

time: 231 us -> 93.3 us (0.40)
  the two profiles are of different devices: /device:TPU:24 before, /device:TPU:20 now
where the time goes in v1:
time: 93.3 us; the launch traced here: 93.8 us
  Pallas kernels  57.4 us (62%)
  starting transfers between devices  19.7 us (21%)
  waiting for transfers between devices  12.6 us (14%)
  local copies, waits for them, and re-layouts  3.07 us (3%)
  between operations  0.96 us (1%)
    pallas_call x4, Pallas kernels, attend(): pl.pallas_call(functools.partial(attend_kernel, setup), grid=(tiles,), in...  40.8 us
    ppermute x18, starting transfers between devices, sent(): return lax.ppermute(block, 'tm', pairs)  19.7 us
    ppermute x18, waiting for transfers between devices, sent(): return lax.ppermute(block, 'tm', pairs)  12.6 us
    pallas_call x2, Pallas kernels, to_cross(): pl.pallas_call(functools.partial(across_kernel, len(tokens)), in_specs=[a...  5.5 us
    pallas_call x1, Pallas kernels, self_mix(): pl.pallas_call(functools.partial(norm_kernel, tuple(digits)), in_specs=[a...  5.18 us
    pallas_call x1, Pallas kernels, stretch_states(): pl.pallas_call(state_kernel, in_specs=[anywhere()] * 2, out_specs=[vmem()...  3.22 us
    pallas_call x1, Pallas kernels, turned_keys(): pl.pallas_call(turn_kernel, in_specs=[smem(), anywhere()], out_specs=anyw...  2.75 us
    unnamed x12, local copies, waits for them, and re-layouts  2.47 us
  transfers between devices with their start and end apart: 18, of which 4 were waited for; matrix products, arithmetic and copies ran while one was open for 1% of the time, Pallas kernels for 41%

profile of v1, /device:TPU:20, one launch (start us, length us, event | category | flops | bytes accessed | tf_op | source)
XLA Modules:
  0.0 93.8 jit_solution(3365169426847759164)
XLA Ops:
  0.6 2.8 %turned_keys.1.refs_5_.refs_0_ = bf16[18,128,128]{2,1,0:T(8,128)(2,1)} custom-call(s32[16]{0:T(128)} %tokens_ref.9, bf16[2240,128]{1,0:T(8,128)(2,1)} %bitcast.39), custom_call_target="tpu_custom_call" | custom-call | bytes 1146 | tf_op jit(solution)/shard_map/turned_keys/pallas_call | solution.py:88
  3.4 0.1 collective-permute-start.5
  3.5 0.5 collective-permute-start.4
  4.0 1.6 %collective-permute-start.3 = (bf16[2240,128]{1,0:T(8,128)(2,1)}, bf16[2240,128]{1,0:T(8,128)(2,1)}, u32[]{:S(2)}, u32[]{:S(2)}) collective-permute-start(bf16[2240,128]{1,0:T(8,128)(2,1)} %bitcast.31), channel_id=1, source_target_pairs={{0,4},{1,5},{2,6},{3,7},{4,8},{5,9},{6,10},{7,11},{8,12},{9,13},{1... | collective-permute-start | bytes 1720328 | tf_op jit(solution)/shard_map/ppermute | solution.py:604
  5.5 3.2 %stretch_states.1 = (f32[18,32,128]{2,1,0:T(8,128)}, bf16[18,32,128]{2,1,0:T(8,128)(2,1)}) custom-call(bf16[2240,384]{1,0:T(8,128)(2,1)} %bitcast.34, bf16[2240,384]{1,0:T(8,128)(2,1)} %bitcast.35), custom_call_target="tpu_custom_call" | custom-call | flops 880803 | bytes 3440 | tf_op jit(solution)/shard_map/stretch_states/pallas_call | solution.py:475
  8.8 0.1 collective-permute-start
  8.8 0.6 collective-permute-start.1
  9.4 0.0 collective-permute-done.5.refs_2_.refs_3_
  9.4 0.0 copy-start.2
  9.4 1.3 %collective-permute-start.2 = (bf16[18,32,128]{2,1,0:T(8,128)(2,1)}, bf16[18,32,128]{2,1,0:T(8,128)(2,1)}, u32[]{:S(2)}, u32[]{:S(2)}) collective-permute-start(bf16[18,32,128]{2,1,0:T(8,128)(2,1)} %get-tuple-element.26.refs_6_), channel_id=1, source_target_pairs={{0,3},{1,2},{2,1},{3,0},{4,7},{5,6},{6,5},{7,4},{8,11},{9,10},{10,... | collective-permute-start | bytes 442376 | tf_op jit(solution)/shard_map/ppermute | solution.py:604
  10.7 9.4 %attend.4 = (f32[3,18,4,256]{3,2,1,0:T(4,128)}, f32[3,6,64,256]{3,2,1,0:T(8,128)}, f32[3,6,64,256]{3,2,1,0:T(8,128)}, f32[3,6,64,256]{3,2,1,0:T(8,128)}) custom-call(s32[16]{0:T(128)} %start_ref.7, s32[16]{0:T(128)} %end_ref.7, s32[16]{0:T(128)} %tokens_ref.9, s32[3,16]{1,0:T(4,128)} %bitcast.40, bf16[2240,384]{1,0:T(8,128)(2,1)} %bitcast.17, ...), custom_call_target="tpu_custom_call" | custom-call | flops 4404019 | bytes 3440 | tf_op jit(solution)/shard_map/attend/pallas_call | solution.py:417
  20.1 0.0 copy-done.2
  20.2 0.0 collective-permute-done.refs_4_.refs_0_
  20.2 0.3 collective-permute-start.9
  20.4 0.0 collective-permute-done.1.refs_5_.refs_1_
  20.5 0.0 collective-permute-done.2.refs_6_.refs_2_
  20.5 0.0 collective-permute-done.4.refs_1_.refs_6_
  20.5 0.0 collective-permute-done.3.up_hbm
  20.5 3.6 %to_cross.2 = (bf16[2240,128]{1,0:T(8,128)(2,1)}, bf16[2240,128]{1,0:T(8,128)(2,1)}, bf16[18,32,128]{2,1,0:T(8,128)(2,1)}) custom-call(bf16[2240,128]{1,0:T(8,128)(2,1)} %bitcast.32, bf16[2240,128]{1,0:T(8,128)(2,1)} %collective-permute-done.3.up_hbm, f32[3,18,4,256]{3,2,1,0:T(4,128)} %get-tuple-element.27.refs_0_.refs_1_.refs_6_, ...), custom_call_target="tpu_custom_call", output_to_operand_aliasing={{1}: (1, {})} | custom-call | bytes 1146 | tf_op jit(solution)/shard_map/to_cross/pallas_call | solution.py:164
  24.1 0.5 collective-permute-start.10
  24.6 0.0 collective-permute-start.11
  24.6 1.7 %collective-permute-start.6 = (bf16[18,32,128]{2,1,0:T(8,128)(2,1)}, bf16[18,32,128]{2,1,0:T(8,128)(2,1)}, u32[]{:S(2)}, u32[]{:S(2)}) collective-permute-start(bf16[18,32,128]{2,1,0:T(8,128)(2,1)} %get-tuple-element.28), channel_id=1, source_target_pairs={{0,4},{1,5},{2,6},{3,7},{4,0},{5,1},{6,2},{7,3},{8,12},{9,13},{10,... | collective-permute-start | bytes 442376 | tf_op jit(solution)/shard_map/ppermute | solution.py:604
  26.3 1.7 %collective-permute-start.7 = (bf16[18,32,128]{2,1,0:T(8,128)(2,1)}, bf16[18,32,128]{2,1,0:T(8,128)(2,1)}, u32[]{:S(2)}, u32[]{:S(2)}) collective-permute-start(bf16[18,32,128]{2,1,0:T(8,128)(2,1)} %get-tuple-element.28), channel_id=1, source_target_pairs={{0,8},{1,9},{2,10},{3,11},{4,12},{5,13},{6,14},{7,15},{8,0},{9,1},... | collective-permute-start | bytes 442376 | tf_op jit(solution)/shard_map/ppermute | solution.py:604
  27.9 8.3 %attend.5 = (f32[3,18,4,256]{3,2,1,0:T(4,128)}, f32[3,6,64,256]{3,2,1,0:T(8,128)}, f32[3,6,64,256]{3,2,1,0:T(8,128)}, f32[3,6,64,256]{3,2,1,0:T(8,128)}) custom-call(s32[16]{0:T(128)} %start_ref.7, s32[16]{0:T(128)} %end_ref.7, s32[16]{0:T(128)} %tokens_ref.9, s32[3,16]{1,0:T(4,128)} %bitcast.41, bf16[2240,384]{1,0:T(8,128)(2,1)} %bitcast.20, ...), custom_call_target="tpu_custom_call" | custom-call | flops 4404019 | bytes 3440 | tf_op jit(solution)/shard_map/attend/pallas_call | solution.py:417
  36.3 3.2 %collective-permute-done.10.refs_0_ = bf16[2240,128]{1,0:T(8,128)(2,1)S(1)} collective-permute-done((bf16[2240,128]{1,0:T(8,128)(2,1)}, bf16[2240,128]{1,0:T(8,128)(2,1)S(1)}, u32[]{:S(2)}, u32[]{:S(2)}) %collective-permute-start.10) | collective-permute-done | bytes 573472 | tf_op jit(solution)/shard_map/ppermute | solution.py:604
  39.4 0.0 copy-start
  39.4 0.0 collective-permute-done.11.refs_1_
  39.4 0.8 copy-done
  40.3 0.0 collective-permute-done.6.refs_3_
  40.3 2.2 %collective-permute-done.7.refs_4_ = bf16[18,32,128]{2,1,0:T(8,128)(2,1)} collective-permute-done((bf16[18,32,128]{2,1,0:T(8,128)(2,1)}, bf16[18,32,128]{2,1,0:T(8,128)(2,1)}, u32[]{:S(2)}, u32[]{:S(2)}) %collective-permute-start.7) | collective-permute-done | bytes 147488 | tf_op jit(solution)/shard_map/ppermute | solution.py:604
  42.4 0.0 collective-permute-done.9.up_hbm
  42.4 0.0 copy-start.1
  42.4 0.0 copy-start.3
  42.4 1.9 %to_cross.3 = (bf16[18,128,128]{2,1,0:T(8,128)(2,1)}, bf16[18,128,128]{2,1,0:T(8,128)(2,1)}) custom-call(bf16[18,128,128]{2,1,0:T(8,128)(2,1)} %after.3.refs_3_.own_hbm, bf16[18,128,128]{2,1,0:T(8,128)(2,1)} %collective-permute-done.9.up_hbm, f32[3,18,4,256]{3,2,1,0:T(4,128)} %get-tuple-element.33.refs_2_.refs_0_.refs_10_, ...), custom_call_target="tpu_custom_call", output_to_operand_aliasing={{1}: (1, {})} | custom-call | bytes 1179 | tf_op jit(solution)/shard_map/to_cross/pallas_call | solution.py:164
  44.3 0.1 collective-permute-start.12
  44.4 0.6 collective-permute-start.13
  45.0 1.3 %collective-permute-start.14 = (bf16[18,128,128]{2,1,0:T(8,128)(2,1)}, bf16[18,128,128]{2,1,0:T(8,128)(2,1)}, u32[]{:S(2)}, u32[]{:S(2)}) collective-permute-start(bf16[18,128,128]{2,1,0:T(8,128)(2,1)} %get-tuple-element.37.refs_4_), channel_id=1, source_target_pairs={{1,2},{3,4},{5,6},{7,8},{9,10},{11,12},{13,14},{17,18},{19,20},{21... | collective-permute-start | bytes 1769480 | tf_op jit(solution)/shard_map/ppermute | solution.py:604
  46.3 0.0 copy-done.1
  46.3 1.5 %collective-permute-start.15 = (bf16[2240,128]{1,0:T(8,128)(2,1)S(1)}, bf16[2240,128]{1,0:T(8,128)(2,1)}, u32[]{:S(2)}, u32[]{:S(2)}) collective-permute-start(bf16[2240,128]{1,0:T(8,128)(2,1)S(1)} %copy-done.1), channel_id=1, source_target_pairs={{1,4},{3,6},{5,8},{7,10},{9,12},{11,14},{17,20},{19,22},{21,24},{2... | collective-permute-start | bytes 1720328 | tf_op jit(solution)/shard_map/ppermute | solution.py:604
  47.7 1.4 %collective-permute-start.8 = (bf16[18,32,128]{2,1,0:T(8,128)(2,1)}, bf16[18,32,128]{2,1,0:T(8,128)(2,1)}, u32[]{:S(2)}, u32[]{:S(2)}) collective-permute-start(bf16[18,32,128]{2,1,0:T(8,128)(2,1)} %get-tuple-element.28), channel_id=1, source_target_pairs={{0,12},{1,13},{2,14},{3,15},{4,8},{5,9},{6,10},{7,11},{8,4},{9,5},... | collective-permute-start | bytes 442376 | tf_op jit(solution)/shard_map/ppermute | solution.py:604
  49.1 0.0 copy-done.3
  49.1 0.6 pad_bitcast_fusion.gain_ref
  49.8 0.0 collective-permute-done.12.refs_5_
  49.8 8.7 %attend.6 = (f32[3,18,4,256]{3,2,1,0:T(4,128)}, f32[3,6,64,256]{3,2,1,0:T(8,128)}, f32[3,6,64,256]{3,2,1,0:T(8,128)}, f32[3,6,64,256]{3,2,1,0:T(8,128)}) custom-call(s32[16]{0:T(128)} %start_ref.7, s32[16]{0:T(128)} %end_ref.7, s32[16]{0:T(128)} %tokens_ref.9, s32[3,16]{1,0:T(4,128)} %bitcast.42, bf16[2240,384]{1,0:T(8,128)(2,1)} %bitcast.23, ...), custom_call_target="tpu_custom_call" | custom-call | flops 13212057 | bytes 3440 | tf_op jit(solution)/shard_map/attend/pallas_call | solution.py:417
  58.5 0.0 collective-permute-done.8.refs_5_
  58.5 5.2 %self_mix.1.refs_3_ = bf16[2240,384]{1,0:T(8,128)(2,1)} custom-call(bf16[2240,384]{1,0:T(8,128)(2,1)} %bitcast.36, f32[18,32,128]{2,1,0:T(8,128)} %get-tuple-element.25.refs_3_.own_ref, f32[18,128]{1,0:T(8,128)} %pad_bitcast_fusion.gain_ref, bf16[18,32,128]{2,1,0:T(8,128)(2,1)} %collective-permute-done.refs_4_.refs_0_, ...), custom_call_target="tpu_custom_call" | custom-call | flops 880803 | bytes 3440 | tf_op jit(solution)/shard_map/self_mix/pallas_call | solution.py:585
  63.7 4.6 %collective-permute-done.15.refs_5_.refs_8_ = bf16[2240,128]{1,0:T(8,128)(2,1)} collective-permute-done((bf16[2240,128]{1,0:T(8,128)(2,1)S(1)}, bf16[2240,128]{1,0:T(8,128)(2,1)}, u32[]{:S(2)}, u32[]{:S(2)}) %collective-permute-start.15) | collective-permute-done | bytes 573472 | tf_op jit(solution)/shard_map/ppermute | solution.py:604
  68.3 0.0 collective-permute-done.13.refs_0_
  68.3 0.0 collective-permute-done.14.refs_4_.refs_5_
  68.3 6.7 %collective-permute-start.16 = (bf16[18,128,128]{2,1,0:T(8,128)(2,1)}, bf16[18,128,128]{2,1,0:T(8,128)(2,1)S(1)}, u32[]{:S(2)}, u32[]{:S(2)}) collective-permute-start(bf16[18,128,128]{2,1,0:T(8,128)(2,1)} %get-tuple-element.43.refs_3_), channel_id=1, source_target_pairs={{0,1},{1,0},{2,3},{3,2},{4,5},{5,4},{6,7},{7,6},{8,9},{9,8},{10,11... | collective-permute-start | bytes 1769480 | tf_op jit(solution)/shard_map/ppermute | solution.py:604
  75.0 0.1 collective-permute-start.17
  75.1 2.6 %collective-permute-done.17.refs_7_ = bf16[2240,128]{1,0:T(8,128)(2,1)S(1)} collective-permute-done((bf16[2240,128]{1,0:T(8,128)(2,1)}, bf16[2240,128]{1,0:T(8,128)(2,1)S(1)}, u32[]{:S(2)}, u32[]{:S(2)}) %collective-permute-start.17) | collective-permute-done | bytes 573472 | tf_op jit(solution)/shard_map/ppermute | solution.py:604
  77.7 0.0 copy-start.5
  77.7 0.0 collective-permute-done.16.refs_4_
  77.7 0.8 copy-done.5
  78.5 0.0 copy-start.4
  78.5 0.8 copy-done.4
  79.3 14.3 %attend.7 = bf16[2240,384]{1,0:T(8,128)(2,1)} custom-call(s32[16]{0:T(128)} %start_ref.7, s32[16]{0:T(128)} %end_ref.7, s32[16]{0:T(128)} %tokens_ref.9, s32[3,16]{1,0:T(4,128)} %bitcast.43, bf16[2240,384]{1,0:T(8,128)(2,1)} %bitcast.26, bf16[2240,384]{1,0:T(8,128)(2,1)} %bitcast.27, bf16[2240,384]{1,0:T(8,128)(2,1)} %bitcast.28, ...), custom_call_target="tpu_custom_call" | custom-call | flops 13212057 | bytes 3440 | tf_op jit(solution)/shard_map/attend/pallas_call | solution.py:417
  (3 shorter events, 0.0 us)
Async XLA Ops:
  3.4 6.0 %collective-permute-start.5 = (bf16[18,128,128]{2,1,0:T(8,128)(2,1)}, bf16[18,128,128]{2,1,0:T(8,128)(2,1)S(1)}, u32[]{:S(2)}, u32[]{:S(2)}) collective-permute-start(bf16[18,128,128]{2,1,0:T(8,128)(2,1)} %turned_keys.1.refs_5_.refs_0_), channel_id=1, source_target_pairs={{0,1},{1,0},{2,3},{3,2},{4,5},{5,4},{6,7},{7,6},{8,9},{9,8},{10,11... | collective-permute-start | bytes 1769480 | tf_op jit(solution)/shard_map/ppermute | solution.py:604
  3.5 17.0 %collective-permute-start.4 = (bf16[2240,128]{1,0:T(8,128)(2,1)}, bf16[2240,128]{1,0:T(8,128)(2,1)}, u32[]{:S(2)}, u32[]{:S(2)}) collective-permute-start(bf16[2240,128]{1,0:T(8,128)(2,1)} %bitcast.30), channel_id=1, source_target_pairs={{0,1},{1,0},{2,3},{3,2},{4,5},{5,4},{6,7},{7,6},{8,9},{9,8},{10,11... | collective-permute-start | bytes 1720328 | tf_op jit(solution)/shard_map/ppermute | solution.py:604
  4.0 16.5 %collective-permute-start.3 = (bf16[2240,128]{1,0:T(8,128)(2,1)}, bf16[2240,128]{1,0:T(8,128)(2,1)}, u32[]{:S(2)}, u32[]{:S(2)}) collective-permute-start(bf16[2240,128]{1,0:T(8,128)(2,1)} %bitcast.31), channel_id=1, source_target_pairs={{0,4},{1,5},{2,6},{3,7},{4,8},{5,9},{6,10},{7,11},{8,12},{9,13},{1... | collective-permute-start | bytes 1720328 | tf_op jit(solution)/shard_map/ppermute | solution.py:604
  8.8 11.4 %collective-permute-start = (bf16[18,32,128]{2,1,0:T(8,128)(2,1)}, bf16[18,32,128]{2,1,0:T(8,128)(2,1)}, u32[]{:S(2)}, u32[]{:S(2)}) collective-permute-start(bf16[18,32,128]{2,1,0:T(8,128)(2,1)} %get-tuple-element.26.refs_6_), channel_id=1, source_target_pairs={{0,1},{1,0},{2,3},{3,2},{4,5},{5,4},{6,7},{7,6},{8,9},{9,8},{10,11... | collective-permute-start | bytes 442376 | tf_op jit(solution)/shard_map/ppermute | solution.py:604
  8.8 11.6 %collective-permute-start.1 = (bf16[18,32,128]{2,1,0:T(8,128)(2,1)}, bf16[18,32,128]{2,1,0:T(8,128)(2,1)}, u32[]{:S(2)}, u32[]{:S(2)}) collective-permute-start(bf16[18,32,128]{2,1,0:T(8,128)(2,1)} %get-tuple-element.26.refs_6_), channel_id=1, source_target_pairs={{0,2},{1,3},{2,0},{3,1},{4,6},{5,7},{6,4},{7,5},{8,10},{9,11},{10,... | collective-permute-start | bytes 442376 | tf_op jit(solution)/shard_map/ppermute | solution.py:604
  9.4 10.7 %copy-start.2 = (bf16[18,128,128]{2,1,0:T(8,128)(2,1)}, bf16[18,128,128]{2,1,0:T(8,128)(2,1)S(1)}, u32[]{:S(2)}) copy-start(bf16[18,128,128]{2,1,0:T(8,128)(2,1)S(1)} %collective-permute-done.5.refs_2_.refs_3_) | copy-start | bytes 1769476
  9.4 11.0 %collective-permute-start.2 = (bf16[18,32,128]{2,1,0:T(8,128)(2,1)}, bf16[18,32,128]{2,1,0:T(8,128)(2,1)}, u32[]{:S(2)}, u32[]{:S(2)}) collective-permute-start(bf16[18,32,128]{2,1,0:T(8,128)(2,1)} %get-tuple-element.26.refs_6_), channel_id=1, source_target_pairs={{0,3},{1,2},{2,1},{3,0},{4,7},{5,6},{6,5},{7,4},{8,11},{9,10},{10,... | collective-permute-start | bytes 442376 | tf_op jit(solution)/shard_map/ppermute | solution.py:604
  20.2 22.3 %collective-permute-start.9 = (bf16[18,128,128]{2,1,0:T(8,128)(2,1)}, bf16[18,128,128]{2,1,0:T(8,128)(2,1)}, u32[]{:S(2)}, u32[]{:S(2)}) collective-permute-start(bf16[18,128,128]{2,1,0:T(8,128)(2,1)} %after.3.refs_3_.own_hbm), channel_id=1, source_target_pairs={{0,4},{1,5},{2,6},{3,7},{4,8},{5,9},{6,10},{7,11},{8,12},{9,13},{1... | collective-permute-start | bytes 1769480 | tf_op jit(solution)/shard_map/ppermute | solution.py:604
  24.1 15.3 %collective-permute-start.10 = (bf16[2240,128]{1,0:T(8,128)(2,1)}, bf16[2240,128]{1,0:T(8,128)(2,1)S(1)}, u32[]{:S(2)}, u32[]{:S(2)}) collective-permute-start(bf16[2240,128]{1,0:T(8,128)(2,1)} %get-tuple-element.29.refs_5_), channel_id=1, source_target_pairs={{0,2},{1,3},{2,0},{3,1},{4,6},{5,7},{6,4},{7,5},{8,10},{9,11},{10,... | collective-permute-start | bytes 1720328 | tf_op jit(solution)/shard_map/ppermute | solution.py:604
  24.6 14.8 %collective-permute-start.11 = (bf16[2240,128]{1,0:T(8,128)(2,1)}, bf16[2240,128]{1,0:T(8,128)(2,1)}, u32[]{:S(2)}, u32[]{:S(2)}) collective-permute-start(bf16[2240,128]{1,0:T(8,128)(2,1)} %get-tuple-element.34.refs_7_), channel_id=1, source_target_pairs={{0,1},{1,0},{2,3},{3,2},{4,5},{5,4},{6,7},{7,6},{8,9},{9,8},{10,11... | collective-permute-start | bytes 1720328 | tf_op jit(solution)/shard_map/ppermute | solution.py:604
  24.6 15.7 %collective-permute-start.6 = (bf16[18,32,128]{2,1,0:T(8,128)(2,1)}, bf16[18,32,128]{2,1,0:T(8,128)(2,1)}, u32[]{:S(2)}, u32[]{:S(2)}) collective-permute-start(bf16[18,32,128]{2,1,0:T(8,128)(2,1)} %get-tuple-element.28), channel_id=1, source_target_pairs={{0,4},{1,5},{2,6},{3,7},{4,0},{5,1},{6,2},{7,3},{8,12},{9,13},{10,... | collective-permute-start | bytes 442376 | tf_op jit(solution)/shard_map/ppermute | solution.py:604
  26.3 16.2 %collective-permute-start.7 = (bf16[18,32,128]{2,1,0:T(8,128)(2,1)}, bf16[18,32,128]{2,1,0:T(8,128)(2,1)}, u32[]{:S(2)}, u32[]{:S(2)}) collective-permute-start(bf16[18,32,128]{2,1,0:T(8,128)(2,1)} %get-tuple-element.28), channel_id=1, source_target_pairs={{0,8},{1,9},{2,10},{3,11},{4,12},{5,13},{6,14},{7,15},{8,0},{9,1},... | collective-permute-start | bytes 442376 | tf_op jit(solution)/shard_map/ppermute | solution.py:604
  39.4 0.8 copy-start
  42.4 3.8 %copy-start.1 = (bf16[2240,128]{1,0:T(8,128)(2,1)S(1)}, bf16[2240,128]{1,0:T(8,128)(2,1)}, u32[]{:S(2)}) copy-start(bf16[2240,128]{1,0:T(8,128)(2,1)} %get-tuple-element.35.refs_1_) | copy-start | bytes 1720324
  42.4 6.7 %copy-start.3 = (f32[2240]{0:T(1024)S(1)}, f32[2240]{0:T(1024)}, u32[]{:S(2)}) copy-start(f32[2240]{0:T(1024)} %param.25) | copy-start | bytes 26884
  44.3 5.4 %collective-permute-start.12 = (bf16[18,128,128]{2,1,0:T(8,128)(2,1)}, bf16[18,128,128]{2,1,0:T(8,128)(2,1)}, u32[]{:S(2)}, u32[]{:S(2)}) collective-permute-start(bf16[18,128,128]{2,1,0:T(8,128)(2,1)} %get-tuple-element.37.refs_4_), channel_id=1, source_target_pairs={{0,1},{1,0},{2,3},{3,2},{4,5},{5,4},{6,7},{7,6},{8,9},{9,8},{10,11... | collective-permute-start | bytes 1769480 | tf_op jit(solution)/shard_map/ppermute | solution.py:604
  44.4 23.9 %collective-permute-start.13 = (bf16[18,128,128]{2,1,0:T(8,128)(2,1)}, bf16[18,128,128]{2,1,0:T(8,128)(2,1)}, u32[]{:S(2)}, u32[]{:S(2)}) collective-permute-start(bf16[18,128,128]{2,1,0:T(8,128)(2,1)} %get-tuple-element.38.refs_9_), channel_id=1, source_target_pairs={{0,2},{1,3},{2,0},{3,1},{4,6},{5,7},{6,4},{7,5},{8,10},{9,11},{10,... | collective-permute-start | bytes 1769480 | tf_op jit(solution)/shard_map/ppermute | solution.py:604
  45.0 23.4 %collective-permute-start.14 = (bf16[18,128,128]{2,1,0:T(8,128)(2,1)}, bf16[18,128,128]{2,1,0:T(8,128)(2,1)}, u32[]{:S(2)}, u32[]{:S(2)}) collective-permute-start(bf16[18,128,128]{2,1,0:T(8,128)(2,1)} %get-tuple-element.37.refs_4_), channel_id=1, source_target_pairs={{1,2},{3,4},{5,6},{7,8},{9,10},{11,12},{13,14},{17,18},{19,20},{21... | collective-permute-start | bytes 1769480 | tf_op jit(solution)/shard_map/ppermute | solution.py:604
  46.3 22.0 %collective-permute-start.15 = (bf16[2240,128]{1,0:T(8,128)(2,1)S(1)}, bf16[2240,128]{1,0:T(8,128)(2,1)}, u32[]{:S(2)}, u32[]{:S(2)}) collective-permute-start(bf16[2240,128]{1,0:T(8,128)(2,1)S(1)} %copy-done.1), channel_id=1, source_target_pairs={{1,4},{3,6},{5,8},{7,10},{9,12},{11,14},{17,20},{19,22},{21,24},{2... | collective-permute-start | bytes 1720328 | tf_op jit(solution)/shard_map/ppermute | solution.py:604
  47.7 10.8 %collective-permute-start.8 = (bf16[18,32,128]{2,1,0:T(8,128)(2,1)}, bf16[18,32,128]{2,1,0:T(8,128)(2,1)}, u32[]{:S(2)}, u32[]{:S(2)}) collective-permute-start(bf16[18,32,128]{2,1,0:T(8,128)(2,1)} %get-tuple-element.28), channel_id=1, source_target_pairs={{0,12},{1,13},{2,14},{3,15},{4,8},{5,9},{6,10},{7,11},{8,4},{9,5},... | collective-permute-start | bytes 442376 | tf_op jit(solution)/shard_map/ppermute | solution.py:604
  68.3 9.3 %collective-permute-start.16 = (bf16[18,128,128]{2,1,0:T(8,128)(2,1)}, bf16[18,128,128]{2,1,0:T(8,128)(2,1)S(1)}, u32[]{:S(2)}, u32[]{:S(2)}) collective-permute-start(bf16[18,128,128]{2,1,0:T(8,128)(2,1)} %get-tuple-element.43.refs_3_), channel_id=1, source_target_pairs={{0,1},{1,0},{2,3},{3,2},{4,5},{5,4},{6,7},{7,6},{8,9},{9,8},{10,11... | collective-permute-start | bytes 1769480 | tf_op jit(solution)/shard_map/ppermute | solution.py:604
  75.0 2.7 %collective-permute-start.17 = (bf16[2240,128]{1,0:T(8,128)(2,1)}, bf16[2240,128]{1,0:T(8,128)(2,1)S(1)}, u32[]{:S(2)}, u32[]{:S(2)}) collective-permute-start(bf16[2240,128]{1,0:T(8,128)(2,1)} %get-tuple-element.44.refs_6_), channel_id=1, source_target_pairs={{0,1},{1,0},{2,3},{3,2},{4,5},{5,4},{6,7},{7,6},{8,9},{9,8},{10,11... | collective-permute-start | bytes 1720328 | tf_op jit(solution)/shard_map/ppermute | solution.py:604
  77.7 0.8 copy-start.5
  78.5 0.8 copy-start.4

commit v2 on v1

--- a/solution.py
+++ b/solution.py
@@ -18,7 +18,7 @@
 STEP = 3
 PARTS = 3
 COPIES = 2
-ROOM = 66_400_000
+ROOM = 66_900_000
 
 
 def vmem():
@@ -56,50 +56,53 @@
     return jnp.where(rows < used, turned, turned[0:1, :]).astype(BF)
 
 
-def turn_kernel(tokens_ref, keys_hbm, out_hbm, keys, out, in_sems, out_sems):
-    used = tokens_ref[lax.axis_index("tm")]
-    width, quads = keys.shape[0], out.shape[0]
+def turn_kernel(tokens_ref, *refs):
+    count = len(refs) // 5
+    keys_hbm, out_hbm, keys, out, sems = (refs[count * k : count * (k + 1)] for k in range(5))
+    width, quads = keys[0].shape[0], out[0].shape[0]
     every = quads // PARTS
     rows = lax.broadcasted_iota(jnp.int32, (QUAD, QUAD), 0)
 
-    def move_in(part):
+    def move_in(n, part):
         at = part_rows(width, quads, part)
-        return pltpu.make_async_copy(keys_hbm.at[at], keys.at[at], in_sems.at[part])
-
-    def move_out(part):
+        return pltpu.make_async_copy(keys_hbm[n].at[at], keys[n].at[at], sems[n].at[0, part])
+
+    def move_out(n, part):
         at = pl.ds(part * every, every)
-        return pltpu.make_async_copy(out.at[at], out_hbm.at[at], out_sems.at[part])
-
-    for part in range(PARTS):
-        move_in(part).start()
-    for q in range(quads):
-        if q % every == 0:
-            move_in(q // every).wait()
-        out[q] = turned_quad(quad_rows(keys, q, width), used, rows)
-        if q % every == every - 1:
-            move_out(q // every).start()
-    for part in range(PARTS):
-        move_out(part).wait()
-
-
-def turned_keys(tokens, keys):
-    width, slots = keys.shape
+        return pltpu.make_async_copy(out[n].at[at], out_hbm[n].at[at], sems[n].at[1, part])
+
+    for n in range(count):
+        for part in range(PARTS):
+            move_in(n, part).start()
+    for n in range(count):
+        used = QUAD if n else tokens_ref[lax.axis_index("tm")]
+        for q in range(quads):
+            if q % every == 0:
+                move_in(n, q // every).wait()
+            out[n][q] = turned_quad(quad_rows(keys[n], q, width), used, rows)
+            if q % every == every - 1:
+                move_out(n, q // every).start()
+    for n in range(count):
+        for part in range(PARTS):
+            move_out(n, part).wait()
+
+
+def turned_keys(tokens, *keys):
+    width, slots = keys[0].shape
     shape = (-(-width // QUAD), slots, QUAD)
+    count = len(keys)
     return pl.pallas_call(
         turn_kernel,
-        in_specs=[smem(), anywhere()],
-        out_specs=anywhere(),
-        out_shape=jax.ShapeDtypeStruct(shape, BF),
-        scratch_shapes=[
-            pltpu.VMEM((width, slots), BF),
-            pltpu.VMEM(shape, BF),
-            pltpu.SemaphoreType.DMA((PARTS,)),
-            pltpu.SemaphoreType.DMA((PARTS,)),
-        ],
+        in_specs=[smem()] + [anywhere()] * count,
+        out_specs=[anywhere()] * count,
+        out_shape=[jax.ShapeDtypeStruct(shape, BF)] * count,
+        scratch_shapes=[pltpu.VMEM((width, slots), BF)] * count
+        + [pltpu.VMEM(shape, BF)] * count
+        + [pltpu.SemaphoreType.DMA((2, PARTS))] * count,
         cost_estimate=cost(0, 4 * width * slots),
         compiler_params=pltpu.CompilerParams(vmem_limit_bytes=ROOM),
         name="turned_keys",
-    )(tokens, keys)
+    )(tokens, *keys)
 
 
 def no_kernel(*refs):
@@ -119,12 +122,7 @@
 
 
 def across_kernel(waits, own_hbm, up_hbm, *refs):
-    *refs, held, in_sems, out_sems = refs[waits:]
-    summed = len(refs) > 2
-    if summed:
-        *states, across_hbm, _, sent_out = refs
-    else:
-        across_hbm, _ = refs
+    across_hbm, _, held, in_sems, out_sems = refs[waits:]
     lower = lax.axis_index("tm") % LAYER < LAYER // 2
     piece = own_hbm.shape[0] // COPIES
 
@@ -146,8 +144,6 @@
         for part in range(COPIES):
             move_in(up_hbm, part).start()
 
-    if summed:
-        digit_step(states[0], states[1:], sent_out)
     for part in range(COPIES):
         move_in(up_hbm, part).wait()
         move_out(part).start()
@@ -155,17 +151,13 @@
         move_out(part).wait()
 
 
-def to_cross(own, up, *tokens, states=()):
+def to_cross(own, up, *tokens):
     shape = jax.ShapeDtypeStruct(own.shape, own.dtype)
-    outs, out_specs = [shape, shape], [anywhere()] * 2
-    if states:
-        outs.append(jax.ShapeDtypeStruct(states[0].shape, BF))
-        out_specs.append(vmem())
     return pl.pallas_call(
         functools.partial(across_kernel, len(tokens)),
-        in_specs=[anywhere()] * (2 + len(tokens)) + [vmem()] * len(states),
-        out_specs=out_specs,
-        out_shape=outs,
+        in_specs=[anywhere()] * (2 + len(tokens)),
+        out_specs=[anywhere()] * 2,
+        out_shape=[shape, shape],
         input_output_aliases={1: 1},
         scratch_shapes=[
             pltpu.VMEM(own.shape, own.dtype),
@@ -175,7 +167,7 @@
         cost_estimate=cost(0, 4 * own.size),
         compiler_params=pltpu.CompilerParams(vmem_limit_bytes=ROOM),
         name="to_cross",
-    )(own, up, *tokens, *states)
+    )(own, up, *tokens)
 
 
 def attend_kernel(setup, start_ref, end_ref, tokens_ref, region_ref, *refs):
@@ -183,31 +175,37 @@
     tile = tokens // tiles
     quads = -(-width // QUAD)
     rounds = quads // STEP
-    every = quads // PARTS
-    query_refs, refs = refs[:PARTS], refs[PARTS:]
-    if first:
-        raw_keys, refs = refs[0], refs[1:]
-    key_hbm = [None] * first + list(refs[: count - first])
-    refs = refs[count - first :]
+    query_hbm, refs = refs[0], refs[1:]
+    key_hbm, refs = refs[:count], refs[count:]
     value_hbm, refs = refs[:count], refs[count + waits :]
     if not first:
-        level_in, total_in = refs[0], refs[1 : 1 + PARTS]
-        refs = refs[1 + PARTS :]
+        state_in, refs = refs[:2], refs[2:]
     if last:
         out_ref, refs = refs[0], refs[1:]
     else:
-        level_out, total_out = refs[0], refs[1 : 1 + PARTS]
-        refs = refs[1 + PARTS :]
-    keys, vals, marks, spread, level, total, s_a, s_b, p_a, p_b, f_a, f_b, work, found, used, ready, sems = refs
+        state_out, refs = refs[:2], refs[2:]
+    keys, vals, marks, queries, spread, levels, totals, level, total, *refs = refs
+    s_a, s_b, p_a, p_b, f_a, f_b, work, found, used, ready, sems, tile_sems = refs
     scale = math.log2(math.e) / math.sqrt(HD)
     none = jnp.zeros((HD, tile), BF)
     i = pl.program_id(0)
 
-    def copies(b):
-        moves = [pltpu.make_async_copy(value_hbm[b], vals.at[b, pl.ds(0, width)], sems.at[b, 1])]
-        if key_hbm[b] is not None:
-            moves.append(pltpu.make_async_copy(key_hbm[b], keys.at[b], sems.at[b, 0]))
-        return moves
+    def copies(b, at):
+        return (
+            pltpu.make_async_copy(key_hbm[b], keys.at[at], sems.at[at, 0]),
+            pltpu.make_async_copy(value_hbm[b], vals.at[at, pl.ds(0, width)], sems.at[at, 1]),
+        )
+
+    def query_move(t):
+        columns = pl.ds(t * tile, tile)
+        return pltpu.make_async_copy(query_hbm.at[:, columns], queries.at[t], tile_sems.at[t, 0])
+
+    def state_moves(t, into):
+        for place, held_here in enumerate((levels, totals)):
+            if into:
+                yield pltpu.make_async_copy(state_in[place].at[t], held_here.at[t], tile_sems.at[t, 1 + place])
+            else:
+                yield pltpu.make_async_copy(held_here.at[t], state_out[place].at[t], tile_sems.at[t, 3 + place])
 
     @pl.when(i == 0)
     def _():
@@ -238,36 +236,39 @@
 
             @pl.when(wanted[b])
             def _():
-                for move in copies(b):
+                for move in copies(b, b):
                     move.start()
 
         for t in range(tiles):
             found[t] = lengths[t]
+
+            @pl.when(lengths[t] > 0)
+            def _():
+                query_move(t).start()
+
+            if not first:
+
+                @pl.when((lengths[t] > 0) | last)
+                def _():
+                    for move in state_moves(t, True):
+                        move.start()
+
         for q in range(quads):
             for h in range(QUAD // HD):
                 off = (1 - h % 2) * tile
                 spread[q, h * HD : (h + 1) * HD, off : off + tile] = none
         lanes = lax.broadcasted_iota(jnp.int32, (16, QUAD), 1)
-        rows = lax.broadcasted_iota(jnp.int32, (QUAD, QUAD), 0)
         for b in range(count):
             marks[b] = jnp.where(lanes < used[b], 1.0, 0.0).astype(BF)
             if width < quads * QUAD:
                 vals[b, width:, :] = jnp.zeros((quads * QUAD - width, QUAD), BF)
-            if key_hbm[b] is None:
-                for q in range(quads):
-                    keys[b, q] = turned_quad(quad_rows(raw_keys, q, width), QUAD, rows)
 
     def arrived(b):
         @pl.when(ready[b] == 0)
         def _():
-            pltpu.make_async_copy(value_hbm[-1], vals.at[b, pl.ds(0, width)], sems.at[b, 1]).wait()
+            for move in copies(0, b):
+                move.wait()
             ready[b] = jnp.int32(1)
-            if key_hbm[-1] is None:
-                return
-
-            @pl.when(b >= first)
-            def _():
-                pltpu.make_async_copy(key_hbm[-1], keys.at[b], sems.at[b, 0]).wait()
 
     low_half = lax.broadcasted_iota(jnp.int32, (QUAD, QUAD), 1) < QUAD // 2
     row16 = lax.broadcasted_iota(jnp.int32, (16, QUAD), 0)
@@ -321,17 +322,21 @@
         level[:, 2:4] = jnp.zeros((quads, 2, 2 * tile), F32)
         total[...] = jnp.zeros(total.shape, F32)
     else:
-        level[...] = level_in[0]
-        for part in range(PARTS):
-            total[part * every : (part + 1) * every] = total_in[part][0]
+
+        @pl.when((n > 0) | last)
+        def _():
+            for move in state_moves(i, True):
+                move.wait()
+            level[...] = levels[i]
+            total[...] = totals[i]
 
     @pl.when(n > 0)
     def _():
+        query_move(i).wait()
         for r in range(0, quads * QUAD, HD):
             q, h = r // QUAD, r % QUAD // HD
             on = h % 2 * tile
-            low = q // every * every * QUAD
-            piece = query_refs[q // every][r - low : r - low + HD, :] if r < width else none
+            piece = queries[i, r : r + HD, :] if r < width else none
             spread[q, h * HD : (h + 1) * HD, on : on + tile] = piece
         b0 = work[i * count]
         arrived(b0)
@@ -368,40 +373,55 @@
                     if r < width:
                         out_ref[r : r + HD, :] = mixed[:, side * tile : (side + 1) * tile].astype(BF)
     else:
-        level_out[0] = level[...]
-        for part in range(PARTS):
-            total_out[part][0] = total[part * every : (part + 1) * every]
+
+        @pl.when((n > 0) | first)
+        def _():
+            levels[i] = level[...]
+            totals[i] = total[...]
+            for move in state_moves(i, False):
+                move.start()
+
+        @pl.when(i == tiles - 1)
+        def _():
+            for t in range(tiles):
+
+                @pl.when((found[t] > 0) | first)
+                def _():
+                    for move in state_moves(t, False):
+                        move.wait()
 
 
 def attend(spans, queries, blocks, held, state, last, waits=()):
     width, tokens = queries.shape
     quads = -(-width // QUAD)
-    every = quads // PARTS
     count = len(blocks)
     tiles, prompts = spans[3].shape
     tile = tokens // tiles
     first = state is None
-    setup = (count, int(first), last, held, len(waits), prompts, width, tokens, tiles)
-    levels, totals = (quads, 4, 2 * tile), (every, 2 * HD, 2 * tile)
-    state_shapes = [(tiles,) + shape for shape in (levels,) + (totals,) * PARTS]
-    state_specs = [pl.BlockSpec((1,) + shape[1:], lambda i: (i, 0, 0, 0)) for shape in state_shapes]
-    query_specs = [pl.BlockSpec((every * QUAD, tile), lambda i, p=p: (p, i)) for p in range(PARTS)]
+    setup = (count, first, last, held, len(waits), prompts, width, tokens, tiles)
+    level, total = (quads, 4, 2 * tile), (quads, 2 * HD, 2 * tile)
+    aliases = {}
     if last:
         outs = [jax.ShapeDtypeStruct((width, tokens), BF)]
         out_specs = [pl.BlockSpec((width, tile), lambda i: (0, i))]
     else:
-        outs = [jax.ShapeDtypeStruct(shape, F32) for shape in state_shapes]
-        out_specs = list(state_specs)
-    raw = [blocks[0][0]] if first else []
-    keys = [block[0] for block in blocks[int(first) :]]
+        outs = [jax.ShapeDtypeStruct((tiles,) + shape, F32) for shape in (level, total)]
+        out_specs = [anywhere()] * 2
+        if not first:
+            at = 5 + 2 * count + len(waits)
+            aliases = {at: 0, at + 1: 1}
+    keys = [block[0] for block in blocks]
     values = [block[1] for block in blocks]
     scratch = [
         pltpu.VMEM((count, quads, QUAD, QUAD), BF),
         pltpu.VMEM((count, quads * QUAD, QUAD), BF),
         pltpu.VMEM((count, 16, QUAD), BF),
+        pltpu.VMEM((tiles, width, tile), BF),
         pltpu.VMEM((quads, QUAD, 2 * tile), BF),
-        pltpu.VMEM(levels, F32),
-        pltpu.VMEM((quads, 2 * HD, 2 * tile), F32),
+        pltpu.VMEM((tiles,) + level, F32),
+        pltpu.VMEM((tiles,) + total, F32),
+        pltpu.VMEM(level, F32),
+        pltpu.VMEM(total, F32),
     ]
     scratch += [pltpu.VMEM((STEP, 2 * QUAD, 2 * tile), F32)] * 2
     scratch += [pltpu.VMEM((STEP, 2 * QUAD, 2 * tile), BF)] * 2
@@ -412,26 +432,23 @@
         pltpu.SMEM((count,), jnp.int32),
         pltpu.SMEM((count,), jnp.int32),
         pltpu.SemaphoreType.DMA((count, 2)),
+        pltpu.SemaphoreType.DMA((tiles, 5)),
     ]
     area = count * QUAD * tokens
     return pl.pallas_call(
         functools.partial(attend_kernel, setup),
         grid=(tiles,),
-        in_specs=[smem()] * 4
-        + query_specs
-        + [pl.BlockSpec(a.shape, lambda i: (0, 0)) for a in raw]
-        + [anywhere()] * (len(keys) + len(values) + len(waits))
-        + state_specs * (not first),
+        in_specs=[smem()] * 4 + [anywhere()] * (1 + 2 * count + len(waits) + (0 if first else 2)),
         out_specs=out_specs,
         out_shape=outs,
         scratch_shapes=scratch,
+        input_output_aliases=aliases,
         cost_estimate=cost(40 * area * width, 4 * width * tokens, area * width // HD),
         compiler_params=pltpu.CompilerParams(vmem_limit_bytes=ROOM),
         name="attend",
     )(
         *spans,
-        *[queries] * PARTS,
-        *raw,
+        queries,
         *keys,
         *values,
         *waits,
@@ -522,7 +539,7 @@
 def digits_of(size):
     hop, digits = 1, []
     while hop < size:
-        radix = 4 if size // hop % 4 == 0 else 2
+        radix = LAYER if hop == 1 and size % LAYER == 0 else 2
         digits.append((hop, radix))
         hop *= radix
     return digits
@@ -569,7 +586,10 @@
     factor = lax.rsqrt(squares / width + 1e-05)
     for q in range(quads):
         size = min(QUAD, width - q * QUAD)
-        gains = jnp.transpose(jnp.broadcast_to(gain_ref[q : q + 1, :], (QUAD, QUAD)))
+        gain = gain_ref[:, q * QUAD : q * QUAD + size]
+        if size < QUAD:
+            gain = jnp.concatenate([gain, jnp.zeros((1, QUAD - size), F32)], axis=1)
+        gains = jnp.transpose(jnp.broadcast_to(gain, (QUAD, QUAD)))
         gains = jnp.concatenate([gains] * (tokens // QUAD), axis=1)
         mixed = (raw[q] * factor * gains).astype(BF)
         out[q * QUAD : q * QUAD + size, :] = mixed[:size]
@@ -597,7 +617,7 @@
         cost_estimate=cost(8 * width * QUAD * tokens, 4 * width * tokens),
         compiler_params=pltpu.CompilerParams(vmem_limit_bytes=ROOM),
         name="self_mix",
-    )(queries, own, jnp.pad(gain, (0, quads * QUAD - width)).reshape(quads, QUAD), *partners, token)
+    )(queries, own, gain, *partners, token)
 
 
 def sent(block, pairs):
@@ -640,49 +660,50 @@
 
     own_v = turned(prompt_values)
     up_v = sent(own_v, up)
-    own_k = turned_keys(prompt_tokens, turned(prompt_keys))
+    own_k, caption_k = turned_keys(prompt_tokens, turned(prompt_keys), jnp.transpose(caption_keys))
+    own_v_beside = sent(own_v, beside)
     own_sums, going = stretch_states(jnp.transpose(keys), jnp.transpose(values))
-    caption = (jnp.transpose(caption_keys), jnp.transpose(caption_values))
-    state = call([caption], lambda c: [None], None, False, waits=[own_k, going])
-
     partners = swapped(going, *digits[0])
-    own_v_beside = sent(own_v, beside)
-    own_k_beside = sent(own_k, beside)
-    across_v, up_v, going = to_cross(
-        own_v, up_v, state[0], own_v_beside, own_k_beside, states=[own_sums, *partners]
-    )
+    state = call([(caption_k, jnp.transpose(caption_values))], lambda c: [None], None, False, waits=[going])
+
+    gain_row = out_gain.reshape(1, width)
+    across_v, up_v = to_cross(own_v, up_v, state[0], own_v_beside, gain_row, *partners)
     swap_v = sent(across_v, swap)
-    (late_k,) = after([own_k], state[0], own_k_beside)
+    (late_k,) = after([own_k], state[0])
     up_k = sent(late_k, up)
+    own_k_beside = sent(late_k, beside)
     up_v_beside = sent(up_v, beside)
     for digit in digits[1:-1]:
-        partners += swapped(going, *digit)
-        going = digit_sums(own_sums, partners, state[0])
-    final = swapped(going, *digits[-1]) if len(digits) > 1 else []
-    state = call([(late_k, own_v)], lambda c: [c], state, False, waits=[across_v])
-
-    swap_v, up_v_beside = after([swap_v, up_v_beside], state[0])
-    across_k, up_k = to_cross(late_k, up_k, state[0], swap_v, up_v_beside, *final[:2])
+        partners += swapped(digit_sums(own_sums, partners, across_v), *digit)
+    state = call(
+        [(late_k, own_v), (own_k_beside, own_v_beside)],
+        lambda c: [c, pick(c, (1, 1), (3, 1))],
+        state,
+        False,
+        waits=[across_v],
+    )
+
+    (swap_v,) = after([swap_v], state[0])
+    across_k, up_k = to_cross(late_k, up_k, state[0], up_v_beside, *partners)
     swap_k = sent(across_k, swap)
     far_k = sent(up_k, further)
     far_v = sent(swap_v, onward)
     up_k_beside = sent(up_k, beside)
+    final = []
+    if len(digits) > 1:
+        final = swapped(digit_sums(own_sums, partners, across_k), *digits[-1])
     state = call(
-        [(own_k_beside, own_v_beside), (up_k, up_v), (up_k_beside, up_v_beside)],
-        lambda c: [
-            pick(c, (1, 1), (3, 1)),
-            c - LAYER,
-            pick(c, (0, 3), (2, 3), (1, 5), (3, 5)),
-        ],
+        [(up_k, up_v), (up_k_beside, up_v_beside)],
+        lambda c: [c - LAYER, pick(c, (0, 3), (2, 3), (1, 5), (3, 5))],
         state,
         False,
         waits=[across_k],
     )
 
-    self_mixed = self_mix(jnp.transpose(queries), own_sums, out_gain, partners + final, digits, state[0])
-    swap_k, swap_v = after([swap_k, swap_v], state[0], self_mixed, far_k, far_v)
+    swap_k, swap_v = after([swap_k, swap_v], state[0], far_k, far_v, *final)
+    swap_k_beside = sent(swap_k, beside)
     swap_v_beside = sent(swap_v, beside)
-    swap_k_beside = sent(swap_k, beside)
+    self_mixed = self_mix(jnp.transpose(queries), own_sums, gain_row, partners + final, digits, swap_k)
     cross_mixed = call(
         [(swap_k, swap_v), (swap_k_beside, swap_v_beside), (far_k, far_v)],
         lambda c: [
@@ -692,6 +713,7 @@
         ],
         state,
         True,
+        waits=[self_mixed],
     )[0]
     return (jnp.transpose(self_mixed), jnp.transpose(cross_mixed))
 

time: 93.3 us -> 86 us (0.922); the launches traced: 93.8 us -> 85.1 us
  starting transfers between devices: 19.7 us -> 15.9 us
  Pallas kernels: 57.4 us -> 54.4 us
  local copies, waits for them, and re-layouts: 3.07 us -> 0.61 us
    pallas_call x4, Pallas kernels: 40.8 us -> 35.3 us  [attend(): pl.pallas_call(functools.partial(attend_kernel, setup), grid=(tiles,), in...]
    pallas_call x1 -> x3, Pallas kernels: 2.75 us -> 7.09 us  [the longest x2 3.82 us: digit_sums(): pl.pallas_call(digit_kernel, in_specs=[vmem()] * (1 + len(partners)) + [a...]
    ppermute x18 -> x17, starting transfers between devices: 19.7 us -> 15.9 us  [sent(): return lax.ppermute(block, 'tm', pairs)]
    unnamed x12 -> x2, local copies, waits for them, and re-layouts: 2.47 us -> 0.01 us
    pallas_call x2, Pallas kernels: 5.5 us -> 3.64 us  [to_cross(): pl.pallas_call(functools.partial(across_kernel, len(tokens)), in_specs=[a...]
    ppermute x18 -> x17, waiting for transfers between devices: 12.6 us -> 13.2 us  [sent(): return lax.ppermute(block, 'tm', pairs)]
  transfers between devices with their start and end apart: 18 -> 17, of which waited for: 4 -> 3; matrix products, arithmetic and copies ran while one was open for 1% -> 1% of each run, Pallas kernels for 41% -> 47%
where the time goes in v2:
time: 86 us; the launch traced here: 85.1 us
  Pallas kernels  54.4 us (63%)
  starting transfers between devices  15.9 us (18%)
  waiting for transfers between devices  13.2 us (15%)
  between operations  0.98 us (1%)
    pallas_call x4, Pallas kernels, attend(): pl.pallas_call(functools.partial(attend_kernel, setup), grid=(tiles,), in...  35.3 us
    ppermute x17, starting transfers between devices, sent(): return lax.ppermute(block, 'tm', pairs)  15.9 us
    ppermute x17, waiting for transfers between devices, sent(): return lax.ppermute(block, 'tm', pairs)  13.2 us
    pallas_call x1, Pallas kernels, self_mix(): pl.pallas_call(functools.partial(norm_kernel, tuple(digits)), in_specs=[a...  5.16 us
    pallas_call x2, Pallas kernels, digit_sums(): pl.pallas_call(digit_kernel, in_specs=[vmem()] * (1 + len(partners)) + [a...  3.82 us
    pallas_call x2, Pallas kernels, to_cross(): pl.pallas_call(functools.partial(across_kernel, len(tokens)), in_specs=[a...  3.64 us
    pallas_call x1, Pallas kernels, turned_keys(): pl.pallas_call(turn_kernel, in_specs=[smem()] + [anywhere()] * count, out...  3.27 us
    pallas_call x1, Pallas kernels, stretch_states(): pl.pallas_call(state_kernel, in_specs=[anywhere()] * 2, out_specs=[vmem()...  3.21 us
  transfers between devices with their start and end apart: 17, of which 3 were waited for; matrix products, arithmetic and copies ran while one was open for 1% of the time, Pallas kernels for 47%

profile of v2, /device:TPU:20, one launch (start us, length us, event | category | flops | bytes accessed | tf_op | source)
XLA Modules:
  0.0 85.1 jit_solution(12363467108487275669)
XLA Ops:
  0.6 0.1 collective-permute-start.4
  0.7 1.6 %collective-permute-start.3 = (bf16[2240,128]{1,0:T(8,128)(2,1)}, bf16[2240,128]{1,0:T(8,128)(2,1)}, u32[]{:S(2)}, u32[]{:S(2)}) collective-permute-start(bf16[2240,128]{1,0:T(8,128)(2,1)} %bitcast.22), channel_id=1, source_target_pairs={{0,4},{1,5},{2,6},{3,7},{4,8},{5,9},{6,10},{7,11},{8,12},{9,13},{1... | collective-permute-start | bytes 1720328 | tf_op jit(solution)/shard_map/ppermute | solution.py:624
  2.3 3.2 %stretch_states.1 = (f32[18,32,128]{2,1,0:T(8,128)}, bf16[18,32,128]{2,1,0:T(8,128)(2,1)}) custom-call(bf16[2240,384]{1,0:T(8,128)(2,1)} %bitcast.15, bf16[2240,384]{1,0:T(8,128)(2,1)} %bitcast.16), custom_call_target="tpu_custom_call" | custom-call | flops 880803 | bytes 3440 | tf_op jit(solution)/shard_map/stretch_states/pallas_call | solution.py:492
  5.6 0.2 collective-permute-start
  5.8 0.5 collective-permute-start.1
  6.3 1.2 %collective-permute-start.2 = (bf16[18,32,128]{2,1,0:T(8,128)(2,1)}, bf16[18,32,128]{2,1,0:T(8,128)(2,1)}, u32[]{:S(2)}, u32[]{:S(2)}) collective-permute-start(bf16[18,32,128]{2,1,0:T(8,128)(2,1)} %get-tuple-element.19.refs_3_), channel_id=1, source_target_pairs={{0,3},{1,2},{2,1},{3,0},{4,7},{5,6},{6,5},{7,4},{8,11},{9,10},{10,... | collective-permute-start | bytes 442376 | tf_op jit(solution)/shard_map/ppermute | solution.py:624
  7.5 3.3 %turned_keys.1 = (bf16[18,128,128]{2,1,0:T(8,128)(2,1)}, bf16[18,128,128]{2,1,0:T(8,128)(2,1)}) custom-call(s32[16]{0:T(128)} %tokens_ref.9, bf16[2240,128]{1,0:T(8,128)(2,1)} %bitcast.19, bf16[2240,128]{1,0:T(8,128)(2,1)} %bitcast.20), custom_call_target="tpu_custom_call" | custom-call | bytes 1146 | tf_op jit(solution)/shard_map/turned_keys/pallas_call | solution.py:94
  10.8 0.0 copy-start
  10.8 9.2 %attend.4 = (f32[3,18,4,256]{3,2,1,0:T(4,128)}, f32[3,18,64,256]{3,2,1,0:T(8,128)}) custom-call(s32[16]{0:T(128)} %start_ref.7, s32[16]{0:T(128)} %end_ref.7, s32[16]{0:T(128)} %tokens_ref.9, s32[3,16]{1,0:T(4,128)} %bitcast.30, bf16[2240,384]{1,0:T(8,128)(2,1)} %bitcast.25, bf16[18,128,128]{2,1,0:T(8,128)(2,1)} %get-tuple-element.20.refs_1_, ...), custom_call_target="tpu_custom_call" | custom-call | flops 4404019 | bytes 3440 | tf_op jit(solution)/shard_map/attend/pallas_call | solution.py:438
  20.0 0.0 collective-permute-done.refs_3_.refs_0_.refs_2_
  20.1 0.5 collective-permute-start.7
  20.6 0.0 collective-permute-done.1.refs_4_.refs_1_.refs_3_
  20.6 0.3 collective-permute-start.6
  20.8 0.0 copy-done
  20.8 0.6 reshape.13.refs_2_.gain_ref
  21.5 0.0 collective-permute-done.2.refs_5_.refs_2_.refs_4_
  21.5 0.0 collective-permute-done.4.refs_1_.refs_4_
  21.5 0.0 collective-permute-done.3.up_hbm
  21.5 1.8 %to_cross.2 = (bf16[2240,128]{1,0:T(8,128)(2,1)}, bf16[2240,128]{1,0:T(8,128)(2,1)}) custom-call(bf16[2240,128]{1,0:T(8,128)(2,1)} %bitcast.23, bf16[2240,128]{1,0:T(8,128)(2,1)} %collective-permute-done.3.up_hbm, f32[3,18,4,256]{3,2,1,0:T(4,128)} %get-tuple-element.21.refs_0_.refs_1_.refs_6_, ...), custom_call_target="tpu_custom_call", output_to_operand_aliasing={{1}: (1, {})} | custom-call | bytes 1146 | tf_op jit(solution)/shard_map/to_cross/pallas_call | solution.py:156
  23.3 0.1 collective-permute-start.8
  23.4 0.6 collective-permute-start.11
  24.0 1.9 %digit_sums.2 = bf16[18,32,128]{2,1,0:T(8,128)(2,1)} custom-call(f32[18,32,128]{2,1,0:T(8,128)} %get-tuple-element.18.own_ref, bf16[18,32,128]{2,1,0:T(8,128)(2,1)} %collective-permute-done.refs_3_.refs_0_.refs_2_, bf16[18,32,128]{2,1,0:T(8,128)(2,1)} %collective-permute-done.1.refs_4_.refs_1_.refs_3_, ...), custom_call_target="tpu_custom_call" | custom-call | bytes 589 | tf_op jit(solution)/shard_map/digit_sums/pallas_call | solution.py:528
  25.8 1.5 %collective-permute-start.5 = (bf16[18,32,128]{2,1,0:T(8,128)(2,1)}, bf16[18,32,128]{2,1,0:T(8,128)(2,1)}, u32[]{:S(2)}, u32[]{:S(2)}) collective-permute-start(bf16[18,32,128]{2,1,0:T(8,128)(2,1)} %digit_sums.2), channel_id=1, source_target_pairs={{0,4},{1,5},{2,6},{3,7},{4,0},{5,1},{6,2},{7,3},{8,12},{9,13},{10,... | collective-permute-start | bytes 442376 | tf_op jit(solution)/shard_map/ppermute | solution.py:624
  27.3 0.0 collective-permute-done.7.refs_2_
  27.3 1.1 %attend.5 = (f32[3,18,4,256]{3,2,1,0:T(4,128)}, f32[3,18,64,256]{3,2,1,0:T(8,128)}) custom-call(s32[16]{0:T(128)} %start_ref.7, s32[16]{0:T(128)} %end_ref.7, s32[16]{0:T(128)} %tokens_ref.9, s32[3,16]{1,0:T(4,128)} %bitcast.31, bf16[2240,384]{1,0:T(8,128)(2,1)} %bitcast.26, ...), custom_call_target="tpu_custom_call", output_to_operand_aliasing={{0}: (10, {}), {1}: (11, {})} | custom-call | flops 8808038 | bytes 3440 | tf_op jit(solution)/shard_map/attend/pallas_call | solution.py:438
  28.5 7.7 %collective-permute-done.6.up_hbm = bf16[18,128,128]{2,1,0:T(8,128)(2,1)} collective-permute-done((bf16[18,128,128]{2,1,0:T(8,128)(2,1)}, bf16[18,128,128]{2,1,0:T(8,128)(2,1)}, u32[]{:S(2)}, u32[]{:S(2)}) %collective-permute-start.6) | collective-permute-done | bytes 589856 | tf_op jit(solution)/shard_map/ppermute | solution.py:624
  36.2 2.9 %collective-permute-done.5.refs_5_.refs_3_ = bf16[18,32,128]{2,1,0:T(8,128)(2,1)} collective-permute-done((bf16[18,32,128]{2,1,0:T(8,128)(2,1)}, bf16[18,32,128]{2,1,0:T(8,128)(2,1)}, u32[]{:S(2)}, u32[]{:S(2)}) %collective-permute-start.5) | collective-permute-done | bytes 147488 | tf_op jit(solution)/shard_map/ppermute | solution.py:624
  39.1 0.0 collective-permute-done.8.refs_1_.refs_4_
  39.1 1.8 %to_cross.3 = (bf16[18,128,128]{2,1,0:T(8,128)(2,1)}, bf16[18,128,128]{2,1,0:T(8,128)(2,1)}) custom-call(bf16[18,128,128]{2,1,0:T(8,128)(2,1)} %after.3.refs_1_.own_hbm, bf16[18,128,128]{2,1,0:T(8,128)(2,1)} %collective-permute-done.6.up_hbm, f32[3,18,4,256]{3,2,1,0:T(4,128)} %get-tuple-element.25.refs_0_.refs_1_.refs_6_, ...), custom_call_target="tpu_custom_call", output_to_operand_aliasing={{1}: (1, {})} | custom-call | bytes 1179 | tf_op jit(solution)/shard_map/to_cross/pallas_call | solution.py:156
  40.9 0.1 collective-permute-start.12
  41.0 0.6 collective-permute-start.10
  41.6 1.3 %collective-permute-start.13 = (bf16[18,128,128]{2,1,0:T(8,128)(2,1)}, bf16[18,128,128]{2,1,0:T(8,128)(2,1)}, u32[]{:S(2)}, u32[]{:S(2)}) collective-permute-start(bf16[18,128,128]{2,1,0:T(8,128)(2,1)} %get-tuple-element.28.refs_1_), channel_id=1, source_target_pairs={{1,2},{3,4},{5,6},{7,8},{9,10},{11,12},{13,14},{17,18},{19,20},{21... | collective-permute-start | bytes 1769480 | tf_op jit(solution)/shard_map/ppermute | solution.py:624
  42.9 0.0 collective-permute-done.11.refs_0_
  42.9 1.5 %collective-permute-start.14 = (bf16[2240,128]{1,0:T(8,128)(2,1)}, bf16[2240,128]{1,0:T(8,128)(2,1)}, u32[]{:S(2)}, u32[]{:S(2)}) collective-permute-start(bf16[2240,128]{1,0:T(8,128)(2,1)} %after.4.refs_1_), channel_id=1, source_target_pairs={{1,4},{3,6},{5,8},{7,10},{9,12},{11,14},{17,20},{19,22},{21,24},{2... | collective-permute-start | bytes 1720328 | tf_op jit(solution)/shard_map/ppermute | solution.py:624
  44.4 1.9 %digit_sums.3 = bf16[18,32,128]{2,1,0:T(8,128)(2,1)} custom-call(f32[18,32,128]{2,1,0:T(8,128)} %get-tuple-element.18.own_ref, bf16[18,32,128]{2,1,0:T(8,128)(2,1)} %collective-permute-done.refs_3_.refs_0_.refs_2_, bf16[18,32,128]{2,1,0:T(8,128)(2,1)} %collective-permute-done.1.refs_4_.refs_1_.refs_3_, ...), custom_call_target="tpu_custom_call" | custom-call | bytes 589 | tf_op jit(solution)/shard_map/digit_sums/pallas_call | solution.py:528
  46.3 5.3 %collective-permute-start.9 = (bf16[18,32,128]{2,1,0:T(8,128)(2,1)}, bf16[18,32,128]{2,1,0:T(8,128)(2,1)}, u32[]{:S(2)}, u32[]{:S(2)}) collective-permute-start(bf16[18,32,128]{2,1,0:T(8,128)(2,1)} %digit_sums.3), channel_id=1, source_target_pairs={{0,8},{1,9},{2,10},{3,11},{4,12},{5,13},{6,14},{7,15},{8,0},{9,1},... | collective-permute-start | bytes 442376 | tf_op jit(solution)/shard_map/ppermute | solution.py:624
  51.7 0.0 collective-permute-done.12.refs_2_
  51.7 10.8 %attend.6 = (f32[3,18,4,256]{3,2,1,0:T(4,128)}, f32[3,18,64,256]{3,2,1,0:T(8,128)}) custom-call(s32[16]{0:T(128)} %start_ref.7, s32[16]{0:T(128)} %end_ref.7, s32[16]{0:T(128)} %tokens_ref.9, s32[3,16]{1,0:T(4,128)} %bitcast.32, bf16[2240,384]{1,0:T(8,128)(2,1)} %bitcast.27, ...), custom_call_target="tpu_custom_call", output_to_operand_aliasing={{0}: (10, {}), {1}: (11, {})} | custom-call | flops 8808038 | bytes 3440 | tf_op jit(solution)/shard_map/attend/pallas_call | solution.py:438
  62.4 0.0 collective-permute-done.9.refs_5_.refs_4_
  62.4 2.5 %collective-permute-done.14.refs_4_.refs_6_ = bf16[2240,128]{1,0:T(8,128)(2,1)} collective-permute-done((bf16[2240,128]{1,0:T(8,128)(2,1)}, bf16[2240,128]{1,0:T(8,128)(2,1)}, u32[]{:S(2)}, u32[]{:S(2)}) %collective-permute-start.14) | collective-permute-done | bytes 573472 | tf_op jit(solution)/shard_map/ppermute | solution.py:624
  65.0 0.0 collective-permute-done.10.refs_0_
  65.0 0.0 collective-permute-done.13.refs_3_
  65.0 0.1 collective-permute-start.15
  65.1 0.5 collective-permute-start.16
  65.6 5.2 %self_mix.1.refs_7_ = bf16[2240,384]{1,0:T(8,128)(2,1)} custom-call(bf16[2240,384]{1,0:T(8,128)(2,1)} %bitcast.17, f32[18,32,128]{2,1,0:T(8,128)} %get-tuple-element.18.own_ref, f32[1,2240]{1,0:T(1,128)} %reshape.13.refs_2_.gain_ref, bf16[18,32,128]{2,1,0:T(8,128)(2,1)} %collective-permute-done.refs_3_.refs_0_.refs_2_, ...), custom_call_target="tpu_custom_call" | custom-call | flops 880803 | bytes 3440 | tf_op jit(solution)/shard_map/self_mix/pallas_call | solution.py:605
  70.7 0.0 collective-permute-done.16.refs_5_
  70.7 0.0 collective-permute-done.15.refs_2_
  70.7 14.2 %attend.7 = bf16[2240,384]{1,0:T(8,128)(2,1)} custom-call(s32[16]{0:T(128)} %start_ref.7, s32[16]{0:T(128)} %end_ref.7, s32[16]{0:T(128)} %tokens_ref.9, s32[3,16]{1,0:T(4,128)} %bitcast.33, bf16[2240,384]{1,0:T(8,128)(2,1)} %bitcast.28, bf16[18,128,128]{2,1,0:T(8,128)(2,1)} %get-tuple-element.31.refs_5_.refs_1_, ...), custom_call_target="tpu_custom_call" | custom-call | flops 13212057 | bytes 3440 | tf_op jit(solution)/shard_map/attend/pallas_call | solution.py:438
  (3 shorter events, 0.0 us)
Async XLA Ops:
  0.6 20.8 %collective-permute-start.4 = (bf16[2240,128]{1,0:T(8,128)(2,1)}, bf16[2240,128]{1,0:T(8,128)(2,1)}, u32[]{:S(2)}, u32[]{:S(2)}) collective-permute-start(bf16[2240,128]{1,0:T(8,128)(2,1)} %bitcast.21), channel_id=1, source_target_pairs={{0,1},{1,0},{2,3},{3,2},{4,5},{5,4},{6,7},{7,6},{8,9},{9,8},{10,11... | collective-permute-start | bytes 1720328 | tf_op jit(solution)/shard_map/ppermute | solution.py:624
  0.7 20.7 %collective-permute-start.3 = (bf16[2240,128]{1,0:T(8,128)(2,1)}, bf16[2240,128]{1,0:T(8,128)(2,1)}, u32[]{:S(2)}, u32[]{:S(2)}) collective-permute-start(bf16[2240,128]{1,0:T(8,128)(2,1)} %bitcast.22), channel_id=1, source_target_pairs={{0,4},{1,5},{2,6},{3,7},{4,8},{5,9},{6,10},{7,11},{8,12},{9,13},{1... | collective-permute-start | bytes 1720328 | tf_op jit(solution)/shard_map/ppermute | solution.py:624
  5.6 14.5 %collective-permute-start = (bf16[18,32,128]{2,1,0:T(8,128)(2,1)}, bf16[18,32,128]{2,1,0:T(8,128)(2,1)}, u32[]{:S(2)}, u32[]{:S(2)}) collective-permute-start(bf16[18,32,128]{2,1,0:T(8,128)(2,1)} %get-tuple-element.19.refs_3_), channel_id=1, source_target_pairs={{0,1},{1,0},{2,3},{3,2},{4,5},{5,4},{6,7},{7,6},{8,9},{9,8},{10,11... | collective-permute-start | bytes 442376 | tf_op jit(solution)/shard_map/ppermute | solution.py:624
  5.8 14.8 %collective-permute-start.1 = (bf16[18,32,128]{2,1,0:T(8,128)(2,1)}, bf16[18,32,128]{2,1,0:T(8,128)(2,1)}, u32[]{:S(2)}, u32[]{:S(2)}) collective-permute-start(bf16[18,32,128]{2,1,0:T(8,128)(2,1)} %get-tuple-element.19.refs_3_), channel_id=1, source_target_pairs={{0,2},{1,3},{2,0},{3,1},{4,6},{5,7},{6,4},{7,5},{8,10},{9,11},{10,... | collective-permute-start | bytes 442376 | tf_op jit(solution)/shard_map/ppermute | solution.py:624
  6.3 15.2 %collective-permute-start.2 = (bf16[18,32,128]{2,1,0:T(8,128)(2,1)}, bf16[18,32,128]{2,1,0:T(8,128)(2,1)}, u32[]{:S(2)}, u32[]{:S(2)}) collective-permute-start(bf16[18,32,128]{2,1,0:T(8,128)(2,1)} %get-tuple-element.19.refs_3_), channel_id=1, source_target_pairs={{0,3},{1,2},{2,1},{3,0},{4,7},{5,6},{6,5},{7,4},{8,11},{9,10},{10,... | collective-permute-start | bytes 442376 | tf_op jit(solution)/shard_map/ppermute | solution.py:624
  10.8 10.1 %copy-start = (f32[2240]{0:T(1024)S(1)}, f32[2240]{0:T(1024)}, u32[]{:S(2)}) copy-start(f32[2240]{0:T(1024)} %param.25) | copy-start | bytes 26884
  20.1 7.3 %collective-permute-start.7 = (bf16[18,128,128]{2,1,0:T(8,128)(2,1)}, bf16[18,128,128]{2,1,0:T(8,128)(2,1)}, u32[]{:S(2)}, u32[]{:S(2)}) collective-permute-start(bf16[18,128,128]{2,1,0:T(8,128)(2,1)} %after.3.refs_1_.own_hbm), channel_id=1, source_target_pairs={{0,1},{1,0},{2,3},{3,2},{4,5},{5,4},{6,7},{7,6},{8,9},{9,8},{10,11... | collective-permute-start | bytes 1769480 | tf_op jit(solution)/shard_map/ppermute | solution.py:624
  20.6 15.6 %collective-permute-start.6 = (bf16[18,128,128]{2,1,0:T(8,128)(2,1)}, bf16[18,128,128]{2,1,0:T(8,128)(2,1)}, u32[]{:S(2)}, u32[]{:S(2)}) collective-permute-start(bf16[18,128,128]{2,1,0:T(8,128)(2,1)} %after.3.refs_1_.own_hbm), channel_id=1, source_target_pairs={{0,4},{1,5},{2,6},{3,7},{4,8},{5,9},{6,10},{7,11},{8,12},{9,13},{1... | collective-permute-start | bytes 1769480 | tf_op jit(solution)/shard_map/ppermute | solution.py:624
  23.3 15.8 %collective-permute-start.8 = (bf16[2240,128]{1,0:T(8,128)(2,1)}, bf16[2240,128]{1,0:T(8,128)(2,1)}, u32[]{:S(2)}, u32[]{:S(2)}) collective-permute-start(bf16[2240,128]{1,0:T(8,128)(2,1)} %get-tuple-element.26.refs_3_), channel_id=1, source_target_pairs={{0,1},{1,0},{2,3},{3,2},{4,5},{5,4},{6,7},{7,6},{8,9},{9,8},{10,11... | collective-permute-start | bytes 1720328 | tf_op jit(solution)/shard_map/ppermute | solution.py:624
  23.4 19.5 %collective-permute-start.11 = (bf16[2240,128]{1,0:T(8,128)(2,1)}, bf16[2240,128]{1,0:T(8,128)(2,1)}, u32[]{:S(2)}, u32[]{:S(2)}) collective-permute-start(bf16[2240,128]{1,0:T(8,128)(2,1)} %get-tuple-element.22.refs_3_.refs_5_), channel_id=1, source_target_pairs={{0,2},{1,3},{2,0},{3,1},{4,6},{5,7},{6,4},{7,5},{8,10},{9,11},{10,... | collective-permute-start | bytes 1720328 | tf_op jit(solution)/shard_map/ppermute | solution.py:624
  25.8 13.3 %collective-permute-start.5 = (bf16[18,32,128]{2,1,0:T(8,128)(2,1)}, bf16[18,32,128]{2,1,0:T(8,128)(2,1)}, u32[]{:S(2)}, u32[]{:S(2)}) collective-permute-start(bf16[18,32,128]{2,1,0:T(8,128)(2,1)} %digit_sums.2), channel_id=1, source_target_pairs={{0,4},{1,5},{2,6},{3,7},{4,0},{5,1},{6,2},{7,3},{8,12},{9,13},{10,... | collective-permute-start | bytes 442376 | tf_op jit(solution)/shard_map/ppermute | solution.py:624
  40.9 10.7 %collective-permute-start.12 = (bf16[18,128,128]{2,1,0:T(8,128)(2,1)}, bf16[18,128,128]{2,1,0:T(8,128)(2,1)}, u32[]{:S(2)}, u32[]{:S(2)}) collective-permute-start(bf16[18,128,128]{2,1,0:T(8,128)(2,1)} %get-tuple-element.28.refs_1_), channel_id=1, source_target_pairs={{0,1},{1,0},{2,3},{3,2},{4,5},{5,4},{6,7},{7,6},{8,9},{9,8},{10,11... | collective-permute-start | bytes 1769480 | tf_op jit(solution)/shard_map/ppermute | solution.py:624
  41.0 24.0 %collective-permute-start.10 = (bf16[18,128,128]{2,1,0:T(8,128)(2,1)}, bf16[18,128,128]{2,1,0:T(8,128)(2,1)}, u32[]{:S(2)}, u32[]{:S(2)}) collective-permute-start(bf16[18,128,128]{2,1,0:T(8,128)(2,1)} %get-tuple-element.27.refs_4_.refs_5_), channel_id=1, source_target_pairs={{0,2},{1,3},{2,0},{3,1},{4,6},{5,7},{6,4},{7,5},{8,10},{9,11},{10,... | collective-permute-start | bytes 1769480 | tf_op jit(solution)/shard_map/ppermute | solution.py:624
  41.6 23.4 %collective-permute-start.13 = (bf16[18,128,128]{2,1,0:T(8,128)(2,1)}, bf16[18,128,128]{2,1,0:T(8,128)(2,1)}, u32[]{:S(2)}, u32[]{:S(2)}) collective-permute-start(bf16[18,128,128]{2,1,0:T(8,128)(2,1)} %get-tuple-element.28.refs_1_), channel_id=1, source_target_pairs={{1,2},{3,4},{5,6},{7,8},{9,10},{11,12},{13,14},{17,18},{19,20},{21... | collective-permute-start | bytes 1769480 | tf_op jit(solution)/shard_map/ppermute | solution.py:624
  42.9 22.1 %collective-permute-start.14 = (bf16[2240,128]{1,0:T(8,128)(2,1)}, bf16[2240,128]{1,0:T(8,128)(2,1)}, u32[]{:S(2)}, u32[]{:S(2)}) collective-permute-start(bf16[2240,128]{1,0:T(8,128)(2,1)} %after.4.refs_1_), channel_id=1, source_target_pairs={{1,4},{3,6},{5,8},{7,10},{9,12},{11,14},{17,20},{19,22},{21,24},{2... | collective-permute-start | bytes 1720328 | tf_op jit(solution)/shard_map/ppermute | solution.py:624
  46.3 16.1 %collective-permute-start.9 = (bf16[18,32,128]{2,1,0:T(8,128)(2,1)}, bf16[18,32,128]{2,1,0:T(8,128)(2,1)}, u32[]{:S(2)}, u32[]{:S(2)}) collective-permute-start(bf16[18,32,128]{2,1,0:T(8,128)(2,1)} %digit_sums.3), channel_id=1, source_target_pairs={{0,8},{1,9},{2,10},{3,11},{4,12},{5,13},{6,14},{7,15},{8,0},{9,1},... | collective-permute-start | bytes 442376 | tf_op jit(solution)/shard_map/ppermute | solution.py:624
  65.0 5.8 %collective-permute-start.15 = (bf16[18,128,128]{2,1,0:T(8,128)(2,1)}, bf16[18,128,128]{2,1,0:T(8,128)(2,1)}, u32[]{:S(2)}, u32[]{:S(2)}) collective-permute-start(bf16[18,128,128]{2,1,0:T(8,128)(2,1)} %get-tuple-element.31.refs_5_.refs_1_), channel_id=1, source_target_pairs={{0,1},{1,0},{2,3},{3,2},{4,5},{5,4},{6,7},{7,6},{8,9},{9,8},{10,11... | collective-permute-start | bytes 1769480 | tf_op jit(solution)/shard_map/ppermute | solution.py:624
  65.1 5.7 %collective-permute-start.16 = (bf16[2240,128]{1,0:T(8,128)(2,1)}, bf16[2240,128]{1,0:T(8,128)(2,1)}, u32[]{:S(2)}, u32[]{:S(2)}) collective-permute-start(bf16[2240,128]{1,0:T(8,128)(2,1)} %get-tuple-element.32.refs_4_), channel_id=1, source_target_pairs={{0,1},{1,0},{2,3},{3,2},{4,5},{5,4},{6,7},{7,6},{8,9},{9,8},{10,11... | collective-permute-start | bytes 1720328 | tf_op jit(solution)/shard_map/ppermute | solution.py:624
